TPU v7x, 32 devices: a whole 2x2x4 slice. The times are simulated.
32 devices in a mesh: dp: 4 (over z), expert: 8 (over y, x, core).
Axes of the slice: x: 2, y: 2, z: 4, core: 2. Of those that a mesh axis runs over, the one named last changes fastest.
Arguments:
- tokens: bfloat16 [4096, 3584], P(('dp', 'expert')), may hold values from -6 to 6
- cotangent: bfloat16 [4096, 3584], P(('dp', 'expert')), may hold values from -6 to 6
- routes: int32 [4096, 1], P(('dp', 'expert')), may hold values from 0 to 7; in each aligned block of 128 rows (0 to 127, 128 to 255, ...) at most 20 rows name the same one
- gates: float32 [4096, 1], P(('dp', 'expert')), may hold values from 0.1 to 1
- w_gate_up: bfloat16 [2, 3584, 8192], P(None, 'dp', 'expert'), may hold values from -0.09375 to 0.09375
- w_down: bfloat16 [8192, 3584], P('expert', 'dp'), may hold values from -0.1875 to 0.1875
- m_gate_up: float32 [2, 3584, 8192], P(None, 'dp', 'expert'), may hold values from -2 to 2
- v_gate_up: float32 [2, 3584, 8192], P(None, 'dp', 'expert'), may hold values from 0.01 to 1
- m_down: float32 [8192, 3584], P('expert', 'dp'), may hold values from -2 to 2
- v_down: float32 [8192, 3584], P('expert', 'dp'), may hold values from 0.01 to 1
Outputs:
- outputs: bfloat16 [4096, 3584], P(('dp', 'expert'))
- input_grads: bfloat16 [4096, 3584], P(('dp', 'expert'))
- new_w_gate_up: bfloat16 [2, 3584, 8192], P(None, 'dp', 'expert')
- new_m_gate_up: float32 [2, 3584, 8192], P(None, 'dp', 'expert')
- new_v_gate_up: float32 [2, 3584, 8192], P(None, 'dp', 'expert')
- new_w_down: bfloat16 [8192, 3584], P('expert', 'dp')
- new_m_down: float32 [8192, 3584], P('expert', 'dp')
- new_v_down: float32 [8192, 3584], P('expert', 'dp')
Inputs may be any that keep to these rules, and one draw needn't show every extreme that they name: `routes`: among the rows of one device, no expert is named more than 20 times, and one expert is named exactly 20 times in some devices' rows.
All inputs are finite; a program needn't handle non-finite values.
Results may differ from a plain program's by a relative error of at most 0.014.
Values may be sent and summed in bfloat16 or wider, within the bound.
A program may use at most 192 MiB of HBM per device.

v0:
```python
import jax
import jax.numpy as jnp
from jax import lax
from jax.sharding import PartitionSpec as P

EXPERTS = 8
CAPACITY = 20


first_decay = 0.9
second_decay = 0.95
first_correction = 1.0 - 0.9**50 * 0.9**50
second_correction = 1.0 - 0.95**50 * 0.95**50
learn_rate = 0.01
adam_epsilon = 1e-08


def slot_positions(flat_routes):
    experts_iota = jnp.arange(EXPERTS, dtype=jnp.int32)
    onehot = (flat_routes[:, None] == experts_iota[None, :]).astype(jnp.int32)
    before = jnp.cumsum(onehot, axis=0) - onehot
    slots = jnp.sum(before * onehot, axis=1)
    return flat_routes * CAPACITY + slots


def adam_update(weight, moment, second, grad_sum, scale):
    grad = grad_sum * scale
    moment_new = first_decay * moment + (1.0 - first_decay) * grad
    second_new = second_decay * second + (1.0 - second_decay) * grad * grad
    update = (
        moment_new / first_correction / (jnp.sqrt(second_new / second_correction) + adam_epsilon)
    )
    weight_new = (weight.astype(jnp.float32) - learn_rate * update).astype(jnp.bfloat16)
    return (weight_new, moment_new, second_new)


def shards(
    tokens, cotangent, routes, gates, w_gate_up, w_down, m_gate_up, v_gate_up, m_down, v_down
):
    n_expert = lax.axis_size("expert")
    n_data = lax.axis_size("dp")
    group = n_expert // EXPERTS
    tok_rows, width = tokens.shape
    topk = routes.shape[1]
    places = slot_positions(routes.reshape(-1))
    gate_flat = gates.reshape(-1)
    token_rows = jnp.repeat(tokens, topk, axis=0)
    cot_rows = (
        gate_flat[:, None] * jnp.repeat(cotangent, topk, axis=0).astype(jnp.float32)
    ).astype(jnp.bfloat16)

    def pack(rows):
        buffer = jnp.zeros((EXPERTS * CAPACITY, width), jnp.bfloat16).at[places].set(rows)
        return jnp.repeat(buffer.reshape(EXPERTS, CAPACITY, width), group, axis=0)

    def unpack(received):
        summed = received.astype(jnp.float32).reshape(EXPERTS, group, CAPACITY, width).sum(axis=1)
        return summed.reshape(EXPERTS * CAPACITY, width)[places].reshape(tok_rows, topk, width)

    weights_up, weights_down = (
        lax.all_gather(w_gate_up, "dp", axis=1, tiled=True),
        lax.all_gather(w_down, "dp", axis=1, tiled=True),
    )
    got_x = lax.all_to_all(pack(token_rows), "expert", split_axis=0, concat_axis=0, tiled=True)
    inputs = got_x.reshape(n_expert * CAPACITY, width)
    pre = jnp.einsum("rc,gcf->grf", inputs, weights_up, preferred_element_type=jnp.float32)
    act_in = pre[0]
    linear = pre[1]
    sig = jax.nn.sigmoid(act_in)
    hidden = (act_in * sig * linear).astype(jnp.bfloat16)
    out_part = jnp.dot(hidden, weights_down, preferred_element_type=jnp.float32).astype(
        jnp.bfloat16
    )
    out_part = out_part.reshape(n_expert, CAPACITY, width)
    back_out = lax.all_to_all(out_part, "expert", split_axis=0, concat_axis=0, tiled=True)
    outputs = jnp.sum(gates[:, :, None] * unpack(back_out), axis=1).astype(jnp.bfloat16)
    got_y = lax.all_to_all(pack(cot_rows), "expert", split_axis=0, concat_axis=0, tiled=True)
    grads_in = got_y.reshape(n_expert * CAPACITY, width)
    d_hidden = lax.dot_general(
        grads_in, weights_down, (((1,), (1,)), ((), ())), preferred_element_type=jnp.float32
    )
    d_act = (d_hidden * linear * sig * (1.0 + act_in * (1.0 - sig))).astype(jnp.bfloat16)
    d_lin = (d_hidden * act_in * sig).astype(jnp.bfloat16)
    d_pre = jnp.stack([d_act, d_lin])
    in_part = jnp.einsum(
        "grf,gcf->rc", d_pre, weights_up, preferred_element_type=jnp.float32
    ).astype(jnp.bfloat16)
    in_part = in_part.reshape(n_expert, CAPACITY, width)
    grad_up = jnp.einsum("rc,grf->gcf", inputs, d_pre, preferred_element_type=jnp.float32)
    grad_down = lax.dot_general(
        hidden, grads_in, (((0,), (0,)), ((), ())), preferred_element_type=jnp.float32
    )
    owned_up, owned_down = (
        lax.psum_scatter(
            grad_up.astype(jnp.bfloat16), "dp", scatter_dimension=1, tiled=True
        ).astype(jnp.float32),
        lax.psum_scatter(
            grad_down.astype(jnp.bfloat16), "dp", scatter_dimension=1, tiled=True
        ).astype(jnp.float32),
    )
    back_in = lax.all_to_all(in_part, "expert", split_axis=0, concat_axis=0, tiled=True)
    input_grads = jnp.sum(unpack(back_in), axis=1).astype(jnp.bfloat16)
    scale = (tok_rows * n_data * n_expert * topk / EXPERTS) ** (-0.5)
    new_wu, new_mu, new_vu = adam_update(w_gate_up, m_gate_up, v_gate_up, owned_up, scale)
    new_wd, new_md, new_vd = adam_update(w_down, m_down, v_down, owned_down, scale)
    return (outputs, input_grads, new_wu, new_mu, new_vu, new_wd, new_md, new_vd)


def solution(mesh):
    placed = (
        P(("dp", "expert"), None),
        P(("dp", "expert"), None),
        P(("dp", "expert"), None),
        P(("dp", "expert"), None),
        P(None, "dp", "expert"),
        P("expert", "dp"),
        P(None, "dp", "expert"),
        P(None, "dp", "expert"),
        P("expert", "dp"),
        P("expert", "dp"),
    )
    return jax.shard_map(
        shards,
        mesh=mesh,
        in_specs=placed,
        out_specs=(
            P(("dp", "expert"), None),
            P(("dp", "expert"), None),
            P(None, "dp", "expert"),
            P(None, "dp", "expert"),
            P(None, "dp", "expert"),
            P("expert", "dp"),
            P("expert", "dp"),
            P("expert", "dp"),
        ),
        check_vma=False,
    )
```

profile of v0, /device:TPU:0, one launch (start us, length us, event | category | flops | bytes accessed | tf_op | source)
XLA Modules:
  0.0 834.2 jit_solution(9907243749834682701)
XLA Ops:
  21.9 15.4 %all-to-all-done = bf16[8,20,3584]{2,1,0:T(8,128)(2,1)S(1)} async-done(((bf16[8,20,3584]{2,1,0:T(8,128)(2,1)}), bf16[8,20,3584]{2,1,0:T(8,128)(2,1)S(1)}, u32[]{:S(2)}, u32[]{:S(2)}) %all-to-all-start) | async-done | bytes 1146912 | tf_op jit(solution)/shard_map/all_to_all | solution.py:64
  41.9 18.6 %all-to-all-done.2 = bf16[8,20,3584]{2,1,0:T(8,128)(2,1)} async-done(((bf16[8,20,3584]{2,1,0:T(8,128)(2,1)}), bf16[8,20,3584]{2,1,0:T(8,128)(2,1)}, u32[]{:S(2)}, u32[]{:S(2)}) %all-to-all-start.2) | async-done | bytes 1146912 | tf_op jit(solution)/shard_map/all_to_all | solution.py:77
  62.8 202.0 %all-gather.3.cloned.1.call-done = bf16[2,3584,1024]{2,1,0:T(8,128)(2,1)} async-done(((bf16[2,896,1024]{2,1,0:T(8,128)(2,1)}), bf16[2,3584,1024]{2,1,0:T(8,128)(2,1)}) %all-gather.3.cloned.1.call-update) | async-done | bytes 14680080 | tf_op jit(solution)/shard_map/all_gather | solution.py:61
  264.8 7.8 convolution_bitcast_fusion.1
  272.6 5.2 convolution_convert_fusion
  277.8 10.4 %copy.38 = bf16[1024,3584]{0,1:T(8,128)(2,1)} copy(bf16[1024,3584]{1,0:T(8,128)(2,1)} %convolution_convert_fusion) | data formatting | bytes 14680064
  288.5 108.6 %all-gather.5.cloned.1.call-done = bf16[1024,3584]{1,0:T(8,128)(2,1)} async-done(((bf16[1024,896]{1,0:T(8,128)(2,1)}), bf16[1024,3584]{1,0:T(8,128)(2,1)}) %all-gather.5.cloned.1.call-update) | async-done | bytes 7340048 | tf_op jit(solution)/shard_map/all_gather | solution.py:62
  397.1 6.0 fusion.26
  403.2 7.3 convert_bitcast_fusion
  410.5 36.6 %copy.36 = bf16[2,3584,1024]{2,0,1:T(2,128)(2,1)} copy(bf16[2,3584,1024]{1,2,0:T(8,128)(2,1)} %convert_bitcast_fusion) | data formatting | bytes 29360128
  447.1 16.1 %copy.40 = bf16[448,8,2,1024]{3,1,2,0:T(8,128)(2,1)} copy(bf16[448,8,2,1024]{3,2,1,0:T(2,128)(2,1)} %bitcast.85) | data formatting | bytes 29360128
  472.7 10.3 %fusion.3 = bf16[160,3584]{1,0:T(8,128)(2,1)S(1)} fusion(bf16[2,3584,1024]{2,1,0:T(8,128)(2,1)} %all-gather.3.cloned.1.call-done, bf16[1,160,1024]{2,1,0:T(8,128)(2,1)S(1)} %get-tuple-element.39, bf16[1,160,1024]{2,1,0:T(8,128)(2,1)S(1)} %get-tuple-element.38), kind=kOutput, calls=%fused_computation.17 | convolution fusion | flops 2349711360 | bytes 16482304 | tf_op jit(solution)/shard_map/grf,gcf->rc/dot_general | solution.py:85
  484.2 7.4 all-to-all-done.1
  496.1 6.0 copy.30
  502.1 8.1 copy.31
  510.3 8.1 copy.32
  532.2 9.0 %subtract_convert_fusion.1 = (bf16[1024,896]{1,0:T(8,128)(2,1)}, f32[1024,896]{1,0:T(8,128)}, f32[1024,896]{1,0:T(8,128)}) fusion(bf16[1024,896]{1,0:T(8,128)(2,1)S(1)} %copy-done, bf16[1024,896]{1,0:T(8,128)(2,1)} %copy.39, f32[1024,896]{1,0:T(8,128)} %param.18, f32[1024,896]{1,0:T(8,128)} %param.19), kind=kLoop, calls=%fused_computation.22 | loop fusion | flops 15597568 | bytes 20185088 | tf_op jit(solution)/shard_map/convert_element_type | solution.py:33
  541.2 232.6 %reduce-scatter.7.cloned.1.call-done = bf16[896,2048]{1,0:T(8,128)(2,1)} async-done(((bf16[3584,2048]{1,0:T(8,128)(2,1)}), bf16[896,2048]{1,0:T(8,128)(2,1)}) %reduce-scatter.7.cloned.1.call-update) | async-done | bytes 3670032
  773.8 7.2 reshape.115
  781.0 10.1 %copy.37 = bf16[2,896,1024]{1,2,0:T(8,128)(2,1)} copy(bf16[2,896,1024]{2,0,1:T(2,128)(2,1)} %bitcast.87) | data formatting | bytes 7340032
  791.1 14.6 %subtract_convert_fusion = (bf16[2,896,1024]{1,2,0:T(8,128)(2,1)}, f32[2,896,1024]{1,2,0:T(8,128)}, f32[2,896,1024]{1,2,0:T(8,128)}) fusion(bf16[2,896,1024]{1,2,0:T(8,128)(2,1)} %copy.30, bf16[2,896,1024]{1,2,0:T(8,128)(2,1)} %copy.37, f32[2,896,1024]{1,2,0:T(8,128)} %copy.31, f32[2,896,1024]{1,2,0:T(8,128)} %copy.32), kind=kLoop, calls=%fused_computation.12 | loop fusion | flops 31195136 | bytes 40370176 | tf_op jit(solution)/shard_map/convert_element_type | solution.py:33
  805.6 6.0 copy.33
  811.6 8.0 copy.34
  819.7 8.0 copy.35
  (46 shorter events, 50.8 us)
Async XLA Ops:
  7.2 1.5 copy-start.4
  7.2 257.6 %all-gather.3.cloned.1.call-start = ((), (), s32[]{:S(2)}) async-start(), calls=%async_computation.6 | async-start | bytes 18350080 | tf_op jit(solution)/shard_map/all_gather | solution.py:61
  7.9 389.2 %all-gather.5.cloned.1.call-start = ((), (), s32[]{:S(2)}) async-start(), calls=%async_computation.7 | async-start | bytes 9175040 | tf_op jit(solution)/shard_map/all_gather | solution.py:62
  8.7 9.7 %copy-start.3 = (bf16[128,3584]{1,0:T(8,128)(2,1)S(1)}, bf16[128,3584]{1,0:T(8,128)(2,1)}, u32[]{:S(2)}) copy-start(bf16[128,3584]{1,0:T(8,128)(2,1)} %param.11) | copy-start | bytes 2752516
  8.7 9.7 %copy-start.5 = (f32[128,1]{0,1:T(1,128)S(1)}, f32[128,1]{0,1:T(1,128)}, u32[]{:S(2)}) copy-start(f32[128,1]{0,1:T(1,128)} %param.13) | copy-start | bytes 1540
  13.2 24.1 %all-to-all-start = ((bf16[8,20,3584]{2,1,0:T(8,128)(2,1)}), bf16[8,20,3584]{2,1,0:T(8,128)(2,1)S(1)}, u32[]{:S(2)}, u32[]{:S(2)}) async-start(bf16[8,20,3584]{2,1,0:T(8,128)(2,1)} %reshape_broadcast_in_dim_reshape.6), calls=%async_computation | async-start | bytes 2752512 | tf_op jit(solution)/shard_map/all_to_all | solution.py:64
  37.3 23.2 %all-to-all-start.2 = ((bf16[8,20,3584]{2,1,0:T(8,128)(2,1)}), bf16[8,20,3584]{2,1,0:T(8,128)(2,1)}, u32[]{:S(2)}, u32[]{:S(2)}) async-start(bf16[8,20,3584]{2,1,0:T(8,128)(2,1)} %reshape_broadcast_in_dim_reshape.7), calls=%async_computation.2 | async-start | bytes 2752512 | tf_op jit(solution)/shard_map/all_to_all | solution.py:77
  41.6 486.8 %reduce-scatter.9.cloned.1.call-start = ((), (), s32[]{:S(2)}) async-start(), calls=%async_computation.9 | async-start | bytes 9175040
  264.8 7.8 copy-start.2
  288.3 485.6 %reduce-scatter.7.cloned.1.call-start = ((), (), s32[]{:S(2)}) async-start(), calls=%async_computation.8 | async-start | bytes 18350080
  469.0 22.6 %all-to-all-start.1 = ((bf16[8,20,3584]{2,1,0:T(8,128)(2,1)}), bf16[8,20,3584]{2,1,0:T(8,128)(2,1)S(1)}, u32[]{:S(2)}, u32[]{:S(2)}) async-start(bf16[8,20,3584]{2,1,0:T(8,128)(2,1)} %reshape.68), calls=%async_computation.1 | async-start | bytes 2752512 | tf_op jit(solution)/shard_map/all_to_all | solution.py:75
  491.6 10.5 %copy-start.1 = (bf16[8,20,3584]{2,1,0:T(8,128)(2,1)}, bf16[8,20,3584]{2,1,0:T(8,128)(2,1)S(1)}, u32[]{:S(2)}) copy-start(bf16[8,20,3584]{2,1,0:T(8,128)(2,1)S(1)} %all-to-all-done.1) | copy-start | bytes 3440644
  491.6 30.6 %all-to-all-start.3 = ((bf16[8,20,3584]{2,1,0:T(8,128)(2,1)}), bf16[8,20,3584]{2,1,0:T(8,128)(2,1)}, u32[]{:S(2)}, u32[]{:S(2)}) async-start(bf16[8,20,3584]{2,1,0:T(8,128)(2,1)} %reshape.72), calls=%async_computation.3 | async-start | bytes 2752512 | tf_op jit(solution)/shard_map/all_to_all | solution.py:101
  525.7 6.5 copy-start
Sparse Core Ops, SparseCore 0:
  9.6 255.1 all-gather.2
  266.4 130.6 all-gather.4
  399.4 125.9 reduce-scatter.8
  527.6 246.1 reduce-scatter.6
where the time goes:
time: 837 us; the launch traced here: 834 us
  waiting for transfers between devices  586 us (70%)
  local copies, waits for them, and re-layouts  146 us (17%)
  matrix products  41.2 us (5%)
  other arithmetic  29 us (3%)
  starting transfers between devices  18 us (2%)
  between operations  13.9 us (2%)
    unnamed x6, waiting for transfers between devices  234 us
    all_gather x1, waiting for transfers between devices, shards(): lax.all_gather(w_gate_up, 'dp', axis=1, tiled=True)  202 us
    unnamed x24, local copies, waits for them, and re-layouts  128 us
    all_gather x1, waiting for transfers between devices, shards(): lax.all_gather(w_down, 'dp', axis=1, tiled=True)  109 us
    convert_element_type x2, other arithmetic, adam_update(): (weight.astype(jnp.float32) - learn_rate * update).astype(jnp.bfloat16)  23.6 us
    all_to_all x1, waiting for transfers between devices, shards(): lax.all_to_all(pack(cot_rows), 'expert', split_axis=0, concat_axis=0, til...  18.6 us
  transfers between devices with their start and end apart: 8, of which 6 were waited for; matrix products, arithmetic and copies ran while one was open for 19% of the time, Pallas kernels for 0%

commit v1 on v0

v1 whole, which is shorter than its diff:
```python
import functools

import jax
import jax.numpy as jnp
from jax import lax
from jax.experimental import pallas as pl
from jax.experimental.pallas import tpu as pltpu
from jax.sharding import PartitionSpec as P

EXPERTS = 8
CAPACITY = 20
BOTH = ("dp", "expert")

first_decay = 0.9
second_decay = 0.95
first_correction = 1.0 - 0.9**50 * 0.9**50
second_correction = 1.0 - 0.95**50 * 0.95**50
learn_rate = 0.01
adam_epsilon = 1e-08
f32, bf16 = jnp.float32, jnp.bfloat16


def selections(routes, group):
    tok, topk = routes.shape
    pairs = tok * topk
    onehot = (routes.reshape(-1)[:, None] == jnp.arange(EXPERTS, dtype=jnp.int32)).astype(f32)
    earlier = (jnp.arange(pairs)[:, None] > jnp.arange(pairs)[None, :]).astype(f32)
    before = jnp.dot(earlier, onehot, preferred_element_type=f32)
    slot = jnp.sum(before * onehot, axis=1)
    at_slot = (slot[:, None] == jnp.arange(CAPACITY, dtype=f32)).astype(f32)
    sel = onehot[:, :, None, None] * at_slot[:, None, None, :]
    sel = jnp.broadcast_to(sel, (pairs, EXPERTS, group, CAPACITY))
    sel = sel.reshape(tok, topk, EXPERTS * group * CAPACITY).astype(bf16)
    return [sel[:, k] for k in range(topk)]


def adam_body(scale, a_ref, b_ref, w_ref, m_ref, v_ref, nw_ref, nm_ref, nv_ref):
    total = lax.dot_general(
        a_ref[...], b_ref[...], (((0,), (0,)), ((), ())), preferred_element_type=f32
    )
    grad = total * scale
    moment = first_decay * m_ref[...] + (1.0 - first_decay) * grad
    second = second_decay * v_ref[...] + (1.0 - second_decay) * grad * grad
    update = moment / first_correction / (jnp.sqrt(second / second_correction) + adam_epsilon)
    nw_ref[...] = (w_ref[...].astype(f32) - learn_rate * update).astype(bf16)
    nm_ref[...] = moment
    nv_ref[...] = second


def grad_adam(a, b, w, m, v, scale):
    rows, width = a.shape
    parts, _, cols = b.shape
    tile = 128 if width % 128 == 0 else width
    state = pl.BlockSpec((None, tile, cols), lambda g, i: (g, i, 0))
    size = parts * width * cols
    return pl.pallas_call(
        functools.partial(adam_body, scale),
        grid=(parts, width // tile),
        in_specs=[
            pl.BlockSpec((rows, tile), lambda g, i: (0, i)),
            pl.BlockSpec((None, rows, cols), lambda g, i: (g, 0, 0)),
            state,
            state,
            state,
        ],
        out_specs=[state, state, state],
        out_shape=[
            jax.ShapeDtypeStruct(w.shape, bf16),
            jax.ShapeDtypeStruct(m.shape, f32),
            jax.ShapeDtypeStruct(v.shape, f32),
        ],
        compiler_params=pltpu.CompilerParams(vmem_limit_bytes=48 * 2**20),
        cost_estimate=pl.CostEstimate(
            flops=2 * rows * size, bytes_accessed=20 * size, transcendentals=2 * size
        ),
        name="grad_adam",
    )(a, b, w, m, v)


def shards(
    tokens, cotangent, routes, gates, w_gate_up, w_down, m_gate_up, v_gate_up, m_down, v_down
):
    n_expert = lax.axis_size("expert")
    n_data = lax.axis_size("dp")
    group = n_expert // EXPERTS
    tok, width = tokens.shape
    topk = routes.shape[1]
    block = width // n_data
    rows = n_data * n_expert * CAPACITY
    sels = selections(routes, group)

    def dispatch(per_choice):
        packed = sum(
            lax.dot_general(s, r, (((0,), (0,)), ((), ())), preferred_element_type=f32)
            for s, r in zip(sels, per_choice)
        ).astype(bf16)
        packed = packed.reshape(n_expert, CAPACITY, n_data, block).transpose(2, 0, 1, 3)
        packed = packed.reshape(n_data * n_expert, CAPACITY, block)
        got = lax.all_to_all(packed, BOTH, split_axis=0, concat_axis=0, tiled=True)
        return got.reshape(rows, block)

    def collect(part):
        part = part.reshape(n_data * n_expert, CAPACITY, block)
        back = lax.all_to_all(part, BOTH, split_axis=0, concat_axis=0, tiled=True)
        back = back.reshape(n_data, n_expert * CAPACITY, block)
        return [
            jnp.einsum("tp,dpc->tdc", s, back, preferred_element_type=f32).reshape(tok, width)
            for s in sels
        ]

    inputs = dispatch([tokens] * topk)
    cot = cotangent.astype(f32)
    grads_in = dispatch([(gates[:, k, None] * cot).astype(bf16) for k in range(topk)])

    pre = jnp.einsum("rc,gcf->rgf", inputs, w_gate_up, preferred_element_type=f32)
    hid = w_gate_up.shape[2]
    pre = lax.psum_scatter(
        pre.astype(bf16).reshape(rows, 2 * hid), "dp", scatter_dimension=0, tiled=True
    ).astype(f32)
    d_hidden = lax.dot_general(
        grads_in, w_down, (((1,), (1,)), ((), ())), preferred_element_type=f32
    )
    d_hidden = lax.psum_scatter(
        d_hidden.astype(bf16), "dp", scatter_dimension=0, tiled=True
    ).astype(f32)
    act_in, linear = pre[:, :hid], pre[:, hid:]
    sig = jax.nn.sigmoid(act_in)
    hidden = (act_in * sig * linear).astype(bf16)
    d_act = (d_hidden * linear * sig * (1.0 + act_in * (1.0 - sig))).astype(bf16)
    d_lin = (d_hidden * act_in * sig).astype(bf16)
    hidden = lax.all_gather(hidden, "dp", axis=0, tiled=True)
    d_pre = lax.all_gather(jnp.stack([d_act, d_lin]), "dp", axis=1, tiled=True)

    out_part = jnp.dot(hidden, w_down, preferred_element_type=f32).astype(bf16)
    outs = collect(out_part)
    outputs = sum(gates[:, k, None] * outs[k] for k in range(topk)).astype(bf16)
    in_part = jnp.einsum("grf,gcf->rc", d_pre, w_gate_up, preferred_element_type=f32).astype(bf16)
    input_grads = sum(collect(in_part)).astype(bf16)

    scale = (tok * n_data * n_expert * topk / EXPERTS) ** (-0.5)
    new_wd, new_md, new_vd = (
        x[0]
        for x in grad_adam(
            hidden, grads_in[None], w_down[None], m_down[None], v_down[None], scale
        )
    )
    new_wu, new_mu, new_vu = grad_adam(inputs, d_pre, w_gate_up, m_gate_up, v_gate_up, scale)
    return (outputs, input_grads, new_wu, new_mu, new_vu, new_wd, new_md, new_vd)


def solution(mesh):
    rows = P(BOTH, None)
    up, down = P(None, "dp", "expert"), P("expert", "dp")
    return jax.shard_map(
        shards,
        mesh=mesh,
        in_specs=(rows, rows, rows, rows, up, down, up, up, down, down),
        out_specs=(rows, rows, up, up, up, down, down, down),
        check_vma=False,
    )
```

time: 837 us -> 351 us (0.42)
  waiting for transfers between devices: 586 us -> 135 us
  local copies, waits for them, and re-layouts: 146 us -> 21.2 us
  blocking collectives: 0 us -> 112 us
  Pallas kernels: 0 us -> 30.5 us
  other arithmetic: 29 us -> 6.36 us
  matrix products: 41.2 us -> 23.3 us
  starting transfers between devices: 18 us -> 7.59 us
    unnamed x6 -> x4, waiting for transfers between devices: 234 us -> 0.07 us
    all_gather x2, waiting for transfers between devices: 311 us -> 105 us  [the longest x1 74.4 us: shards(): d_pre = lax.all_gather(jnp.stack([d_act, d_lin]), 'dp', axis=1, tiled=True)]
    unnamed x24 -> x20, local copies, waits for them, and re-layouts: 128 us -> 3.95 us
    all_to_all x0 -> x2, blocking collectives: none -> 112 us  [dispatch(): got = lax.all_to_all(packed, BOTH, split_axis=0, concat_axis=0, tiled=True)]
    all_to_all x4 -> x2, waiting for transfers between devices: 41.4 us -> 0.01 us  [collect(): back = lax.all_to_all(part, BOTH, split_axis=0, concat_axis=0, tiled=True)]
    pallas_call x0 -> x2, Pallas kernels: none -> 30.5 us  [grad_adam(): pl.pallas_call(functools.partial(adam_body, scale), grid=(parts, width //...]
    reduce_scatter x0 -> x2, waiting for transfers between devices: none -> 29.5 us  [the longest x1 29.5 us: shards(): lax.psum_scatter(d_hidden.astype(bf16), 'dp', scatter_dimension=0, tiled=...]
    convert_element_type x4, other arithmetic: 26.4 us -> 2.99 us  [the longest x1 2.29 us: shards(): pre = lax.psum_scatter(pre.astype(bf16).reshape(rows, 2 * hid), 'dp', sca...]
  transfers between devices with their start and end apart: 8 -> 6, of which waited for: 6 -> 3; matrix products, arithmetic and copies ran while one was open for 19% -> 9% of each run, Pallas kernels for 0% -> 9%
where the time goes in v1:
time: 351 us; the launch traced here: 350 us
  waiting for transfers between devices  135 us (38%)
  blocking collectives  112 us (32%)
  Pallas kernels  30.5 us (9%)
  matrix products  23.3 us (7%)
  local copies, waits for them, and re-layouts  21.2 us (6%)
  between operations  14 us (4%)
  starting transfers between devices  7.59 us (2%)
  other arithmetic  6.36 us (2%)
    all_to_all x2, blocking collectives, dispatch(): got = lax.all_to_all(packed, BOTH, split_axis=0, concat_axis=0, tiled=True)  112 us
    all_gather x1, waiting for transfers between devices, shards(): d_pre = lax.all_gather(jnp.stack([d_act, d_lin]), 'dp', axis=1, tiled=True)  74.4 us
    all_gather x1, waiting for transfers between devices, shards(): hidden = lax.all_gather(hidden, 'dp', axis=0, tiled=True)  30.7 us
    pallas_call x2, Pallas kernels, grad_adam(): pl.pallas_call(functools.partial(adam_body, scale), grid=(parts, width //...  30.5 us
    reduce_scatter x1, waiting for transfers between devices, shards(): lax.psum_scatter(d_hidden.astype(bf16), 'dp', scatter_dimension=0, tiled=...  29.5 us
    all_to_all x2, starting transfers between devices, collect(): back = lax.all_to_all(part, BOTH, split_axis=0, concat_axis=0, tiled=True)  7.42 us
  transfers between devices with their start and end apart: 6, of which 3 were waited for; matrix products, arithmetic and copies ran while one was open for 9% of the time, Pallas kernels for 9%

profile of v1, /device:TPU:0, one launch (start us, length us, event | category | flops | bytes accessed | tf_op | source)
XLA Modules:
  0.0 350.0 jit_solution(18061827677545605711)
XLA Ops:
  9.8 41.6 %all_to_all.20 = bf16[32,20,896]{2,1,0:T(8,128)(2,1)S(1)} all-to-all(bf16[32,20,896]{2,1,0:T(8,128)(2,1)S(1)} %bitcast.46), channel_id=1, replica_groups=mesh['dp'=4,'expert'=8] {'dp','expert'}, dimensions={0} | all-to-all | bytes 2293760 | tf_op jit(solution)/shard_map/all_to_all | solution.py:99
  51.6 5.3 %convert_bitcast_fusion = bf16[2,80,8,1024]{3,2,1,0:T(8,128)(2,1)S(1)} fusion(bf16[640,896,1]{1,0,2:T(8,128)(2,1)S(1)} %reshape.141, bf16[2,896,1024]{2,1,0:T(8,128)(2,1)} %w_ref.1), kind=kOutput, calls=%fused_computation.5 | convolution fusion | flops 2350120960 | bytes 7438336 | tf_op jit(solution)/shard_map/rc,gcf->rgf/dot_general | solution.py:115
  57.0 1.8 copy.27
  60.9 70.9 %all_to_all.21 = bf16[32,20,896]{2,1,0:T(8,128)(2,1)} all-to-all(bf16[32,20,896]{2,1,0:T(8,128)(2,1)S(1)} %bitcast.47), channel_id=1, replica_groups=mesh['dp'=4,'expert'=8] {'dp','expert'}, dimensions={0} | all-to-all | bytes 2293760 | tf_op jit(solution)/shard_map/all_to_all | solution.py:99
  131.9 3.1 reshape.138
  134.9 3.9 %convolution_convert_fusion.3 = bf16[640,1024]{1,0:T(8,128)(2,1)} fusion(bf16[640,896]{1,0:T(8,128)(2,1)} %reshape.138, bf16[1024,896]{1,0:T(8,128)(2,1)S(1)} %copy-done.3), kind=kOutput, calls=%fused_computation.8 | convolution fusion | flops 1175060480 | bytes 4292608 | tf_op jit(solution)/shard_map/dot_general | solution.py:120
  138.9 2.3 convert_element_type.92
  141.2 29.5 %reduce-scatter.5.cloned.1.call-done = bf16[160,1024]{1,0:T(8,128)(2,1)} async-done(((bf16[640,1024]{1,0:T(8,128)(2,1)}), bf16[160,1024]{1,0:T(8,128)(2,1)}) %reduce-scatter.5.cloned.1.call-update) | async-done | bytes 327696 | tf_op jit(solution)/shard_map/reduce_scatter | solution.py:123
  170.7 2.5 fusion.9
  174.2 30.7 %all-gather.3.cloned.1.call-done.a_ref = bf16[640,1024]{1,0:T(8,128)(2,1)} async-done(((bf16[160,1024]{1,0:T(8,128)(2,1)}), bf16[640,1024]{1,0:T(8,128)(2,1)}) %all-gather.3.cloned.1.call-update) | async-done | bytes 1310736 | tf_op jit(solution)/shard_map/all_gather | solution.py:131
  204.8 3.8 %convolution_convert_fusion.4 = bf16[640,896]{1,0:T(8,128)(2,1)} fusion(bf16[640,1024]{1,0:T(8,128)(2,1)} %all-gather.3.cloned.1.call-done.a_ref, bf16[1024,896]{1,0:T(8,128)(2,1)S(1)} %copy-done.3), kind=kOutput, calls=%fused_computation.9 | convolution fusion | flops 1174978560 | bytes 4292608 | tf_op jit(solution)/shard_map/dot_general | solution.py:134
  208.7 2.9 reshape.134
  211.6 3.7 %all-to-all-start.1 = ((bf16[32,20,896]{2,1,0:T(8,128)(2,1)}), bf16[32,20,896]{2,1,0:T(8,128)(2,1)}, u32[]{:S(2)}, u32[]{:S(2)}) async-start(bf16[32,20,896]{2,1,0:T(8,128)(2,1)} %reshape.134), calls=%async_computation.2 | async-start | bytes 2752512 | tf_op jit(solution)/shard_map/all_to_all | solution.py:104
  215.3 74.4 %all-gather.5.cloned.1.call-done.b_ref = bf16[2,640,1024]{2,1,0:T(8,128)(2,1)} async-done(((bf16[2,160,1024]{2,1,0:T(8,128)(2,1)}), bf16[2,640,1024]{2,1,0:T(8,128)(2,1)}) %all-gather.5.cloned.1.call-update) | async-done | bytes 2621456 | tf_op jit(solution)/shard_map/all_gather | solution.py:132
  289.7 5.7 %bitcast_convert_fusion = bf16[640,896]{1,0:T(8,128)(2,1)S(1)} fusion(bf16[2,640,1024]{2,1,0:T(8,128)(2,1)} %all-gather.5.cloned.1.call-done.b_ref, bf16[2,896,1024]{2,1,0:T(8,128)(2,1)} %w_ref.1), kind=kOutput, calls=%fused_computation.6 | convolution fusion | flops 2349383680 | bytes 7438336 | tf_op jit(solution)/shard_map/grf,gcf->rc/dot_general | solution.py:137
  296.7 3.7 %all-to-all-start.3 = ((bf16[32,20,896]{2,1,0:T(8,128)(2,1)}), bf16[32,20,896]{2,1,0:T(8,128)(2,1)}, u32[]{:S(2)}, u32[]{:S(2)}) async-start(bf16[32,20,896]{2,1,0:T(8,128)(2,1)} %reshape.139), calls=%async_computation.5 | async-start | bytes 2752512 | tf_op jit(solution)/shard_map/all_to_all | solution.py:104
  300.7 2.2 broadcast_in_dim_reshape.3.b_ref
  302.9 1.5 copy-done.4
  305.7 10.5 %grad_adam.3 = (bf16[1,1024,896]{2,1,0:T(8,128)(2,1)}, f32[1,1024,896]{2,1,0:T(8,128)}, f32[1,1024,896]{2,1,0:T(8,128)}) custom-call(bf16[640,1024]{1,0:T(8,128)(2,1)S(1)} %copy-done.5, bf16[1,640,896]{2,1,0:T(8,128)(2,1)S(1)} %broadcast_in_dim_reshape.3.b_ref, bf16[1,1024,896]{2,1,0:T(8,128)(2,1)S(1)} %bitcast.44, f32[1,1024,896]{2,1,0:T(8,128)} %bitcast.54, ...), custom_call_target="tpu_custom_call" | custom-call | flops 1174405120 | bytes 18350080 | tf_op jit(solution)/shard_map/grad_adam/pallas_call | solution.py:56
  316.2 20.0 %grad_adam.2 = (bf16[2,896,1024]{2,1,0:T(8,128)(2,1)}, f32[2,896,1024]{2,1,0:T(8,128)}, f32[2,896,1024]{2,1,0:T(8,128)}) custom-call(bf16[640,896]{1,0:T(8,128)(2,1)S(1)} %reshape.132.a_ref, bf16[2,640,1024]{2,1,0:T(8,128)(2,1)S(1)} %copy-done.2, bf16[2,896,1024]{2,1,0:T(8,128)(2,1)} %w_ref.1, f32[2,896,1024]{2,1,0:T(8,128)} %m_ref.1, f32[2,896,1024]{2,1,0:T(8,128)} %v_ref.1), custom_call_target="tpu_custom_call" | custom-call | flops 2348810240 | bytes 36700160 | tf_op jit(solution)/shard_map/grad_adam/pallas_call | solution.py:56
  336.2 2.2 reshape.135
  338.5 1.4 fusion
  339.9 2.2 reshape.140
  342.2 1.3 convolution_convert_fusion.2
  (47 shorter events, 9.1 us)
Async XLA Ops:
  7.2 1.7 copy-start
  7.2 131.7 %reduce-scatter.3.cloned.1.call-start = ((), (), s32[]{:S(2)}) async-start(), calls=%async_computation.6 | async-start | bytes 3276800 | tf_op jit(solution)/shard_map/reduce_scatter | solution.py:117
  51.4 5.6 %copy-start.6 = (bf16[32,20,896]{2,1,0:T(8,128)(2,1)}, bf16[32,20,896]{2,1,0:T(8,128)(2,1)S(1)}, u32[]{:S(2)}) copy-start(bf16[32,20,896]{2,1,0:T(8,128)(2,1)S(1)} %all_to_all.20) | copy-start | bytes 3440644
  58.7 1.2 copy-start.8
  58.7 1.2 copy-start.9
  58.8 111.9 %reduce-scatter.5.cloned.1.call-start = ((), (), s32[]{:S(2)}) async-start(), calls=%async_computation.8 | async-start | bytes 1638400 | tf_op jit(solution)/shard_map/reduce_scatter | solution.py:123
  131.8 3.1 copy-start.3
  138.8 66.0 %all-gather.3.cloned.1.call-start = ((), (), s32[]{:S(2)}) async-start(), calls=%async_computation.7 | async-start | bytes 1638400 | tf_op jit(solution)/shard_map/all_gather | solution.py:131
  173.2 116.5 %all-gather.5.cloned.1.call-start = ((), (), s32[]{:S(2)}) async-start(), calls=%async_computation.9 | async-start | bytes 3276800 | tf_op jit(solution)/shard_map/all_gather | solution.py:132
  211.6 85.0 %all-to-all-start.1 = ((bf16[32,20,896]{2,1,0:T(8,128)(2,1)}), bf16[32,20,896]{2,1,0:T(8,128)(2,1)}, u32[]{:S(2)}, u32[]{:S(2)}) async-start(bf16[32,20,896]{2,1,0:T(8,128)(2,1)} %reshape.134), calls=%async_computation.2 | async-start | bytes 2752512 | tf_op jit(solution)/shard_map/all_to_all | solution.py:104
  296.7 3.7 %copy-start.7 = (bf16[32,20,896]{2,1,0:T(8,128)(2,1)S(1)}, bf16[32,20,896]{2,1,0:T(8,128)(2,1)}, u32[]{:S(2)}) copy-start(bf16[32,20,896]{2,1,0:T(8,128)(2,1)} %copy-done.6) | copy-start | bytes 3440644
  296.7 43.2 %all-to-all-start.3 = ((bf16[32,20,896]{2,1,0:T(8,128)(2,1)}), bf16[32,20,896]{2,1,0:T(8,128)(2,1)}, u32[]{:S(2)}, u32[]{:S(2)}) async-start(bf16[32,20,896]{2,1,0:T(8,128)(2,1)} %reshape.139), calls=%async_computation.5 | async-start | bytes 2752512 | tf_op jit(solution)/shard_map/all_to_all | solution.py:104
  302.9 1.5 copy-start.4
  304.4 1.3 copy-start.5
  305.7 10.5 %copy-start.2 = (bf16[2,640,1024]{2,1,0:T(8,128)(2,1)S(1)}, bf16[2,640,1024]{2,1,0:T(8,128)(2,1)}, u32[]{:S(2)}) copy-start(bf16[2,640,1024]{2,1,0:T(8,128)(2,1)} %all-gather.5.cloned.1.call-done.b_ref) | copy-start | bytes 7864324
  342.1 1.5 copy-start.1
Sparse Core Ops, SparseCore 0:
  58.9 74.0 reduce-scatter.2
  138.9 31.7 reduce-scatter.4
  173.3 31.4 all-gather.2
  206.8 82.8 all-gather.4

commit v2 on v1

--- a/solution.py
+++ b/solution.py
@@ -47,9 +47,9 @@
     nv_ref[...] = second
 
 
-def grad_adam(a, b, w, m, v, scale):
-    rows, width = a.shape
-    parts, _, cols = b.shape
+def grad_adam(a, b, first, w, m, v, scale):
+    rows = a.shape[0]
+    parts, width, cols = w.shape
     tile = 128 if width % 128 == 0 else width
     state = pl.BlockSpec((None, tile, cols), lambda g, i: (g, i, 0))
     size = parts * width * cols
@@ -58,7 +58,7 @@
         grid=(parts, width // tile),
         in_specs=[
             pl.BlockSpec((rows, tile), lambda g, i: (0, i)),
-            pl.BlockSpec((None, rows, cols), lambda g, i: (g, 0, 0)),
+            pl.BlockSpec((rows, cols), lambda g, i: (0, first + g)),
             state,
             state,
             state,
@@ -77,6 +77,155 @@
     )(a, b, w, m, v)
 
 
+SKEW = 2
+
+
+def line_body(n, chunk, count, ab_ref, g_ref, out_ref, sums, got, send, recv):
+    d = lax.axis_index("dp")
+    last = n - 1
+    hid = g_ref.shape[1]
+    half = chunk * count
+    has_low, has_high = d > 0, d < last
+
+    barrier = pltpu.get_barrier_semaphore()
+    for present, peer in ((has_low, d - 1), (has_high, d + 1)):
+
+        @pl.when(present)
+        def _():
+            pl.semaphore_signal(
+                barrier, inc=1, device_id={"dp": peer}, device_id_type=pl.DeviceIdType.MESH
+            )
+
+    pl.semaphore_wait(barrier, has_low.astype(jnp.int32) + has_high.astype(jnp.int32))
+
+    peers = (d + 1, d - 1)
+    starts = (d == 0, d == last)
+    ends = (d == last, d == 0)
+
+    def rows_of(w, c):
+        return pl.ds(pl.multiple_of(w * half + c * chunk, 16), chunk)
+
+    def sum_copy(w, c):
+        return pltpu.make_async_remote_copy(
+            src_ref=sums.at[rows_of(w, c), :],
+            dst_ref=got.at[rows_of(w, c), :],
+            send_sem=send.at[w, c],
+            recv_sem=recv.at[w, c],
+            device_id={"dp": peers[w]},
+            device_id_type=pl.DeviceIdType.MESH,
+        )
+
+    def result_copy(w, c):
+        return pltpu.make_async_remote_copy(
+            src_ref=out_ref.at[rows_of(w, c), :],
+            dst_ref=out_ref.at[rows_of(w, c), :],
+            send_sem=send.at[2 + w, c],
+            recv_sem=recv.at[2 + w, c],
+            device_id={"dp": peers[1 - w]},
+            device_id_type=pl.DeviceIdType.MESH,
+        )
+
+    def step(s, carry):
+        for w in range(2):
+            place = d if w == 0 else last - d
+            c = s - SKEW * place
+
+            @pl.when((c >= 0) & (c < count))
+            def _():
+                rows = rows_of(w, c)
+
+                @pl.when(starts[w])
+                def _():
+                    sums[rows, : 2 * hid] = ab_ref[rows, :]
+                    sums[rows, 2 * hid :] = g_ref[rows, :]
+                    sum_copy(w, c).start()
+
+                @pl.when(jnp.logical_not(starts[w]))
+                def _():
+                    sum_copy(w, c).wait_recv()
+
+                @pl.when(jnp.logical_not(starts[w] | ends[w]))
+                def _():
+                    sums[rows, : 2 * hid] = (
+                        got[rows, : 2 * hid].astype(f32) + ab_ref[rows, :].astype(f32)
+                    ).astype(bf16)
+                    sums[rows, 2 * hid :] = (
+                        got[rows, 2 * hid :].astype(f32) + g_ref[rows, :].astype(f32)
+                    ).astype(bf16)
+                    sum_copy(w, c).start()
+
+                @pl.when(ends[w])
+                def _():
+                    a = got[rows, :hid].astype(f32) + ab_ref[rows, :hid].astype(f32)
+                    b = got[rows, hid : 2 * hid].astype(f32) + ab_ref[rows, hid:].astype(f32)
+                    g = got[rows, 2 * hid :].astype(f32) + g_ref[rows, :].astype(f32)
+                    sig = jax.nn.sigmoid(a)
+                    out_ref[rows, :hid] = (a * sig * b).astype(bf16)
+                    out_ref[rows, hid : 2 * hid] = (
+                        g * b * sig * (1.0 + a * (1.0 - sig))
+                    ).astype(bf16)
+                    out_ref[rows, 2 * hid :] = (g * a * sig).astype(bf16)
+                    result_copy(w, c).start()
+
+        for w in range(2):
+            place = d if w == 0 else last - d
+            c = s - SKEW * (2 * last - place)
+
+            @pl.when((c >= 0) & (c < count) & jnp.logical_not(ends[w]))
+            def _():
+                result_copy(w, c).wait_recv()
+
+                @pl.when(jnp.logical_not(starts[w]))
+                def _():
+                    result_copy(w, c).start()
+
+        return carry
+
+    lax.fori_loop(0, count + 2 * SKEW * last, step, 0)
+
+    def drain(c, carry):
+        for w in range(2):
+
+            @pl.when(jnp.logical_not(ends[w]))
+            def _():
+                sum_copy(w, c).wait_send()
+
+            @pl.when(jnp.logical_not(starts[w]))
+            def _():
+                result_copy(w, c).wait_send()
+
+        return carry
+
+    lax.fori_loop(0, count, drain, 0)
+
+
+def line_activations(ab, g, n):
+    rows, hid = g.shape
+    half = rows // 2
+    count = max(c for c in range(1, 21) if half % (16 * c) == 0)
+    whole = pl.BlockSpec(memory_space=pltpu.VMEM)
+    full = jax.ShapeDtypeStruct((rows, 3 * hid), bf16)
+    return pl.pallas_call(
+        functools.partial(line_body, n, half // count, count),
+        out_shape=full,
+        in_specs=[whole, whole],
+        out_specs=whole,
+        scratch_shapes=[
+            pltpu.VMEM(full.shape, bf16),
+            pltpu.VMEM(full.shape, bf16),
+            pltpu.SemaphoreType.DMA((4, count)),
+            pltpu.SemaphoreType.DMA((4, count)),
+        ],
+        compiler_params=pltpu.CompilerParams(
+            collective_id=0, has_side_effects=True, vmem_limit_bytes=56 * 2**20
+        ),
+        cost_estimate=pl.CostEstimate(
+            flops=30 * rows * hid, bytes_accessed=12 * rows * hid, transcendentals=rows * hid
+        ),
+        name="line_activations",
+    )(ab, g)
+
+
 def shards(
     tokens, cotangent, routes, gates, w_gate_up, w_down, m_gate_up, v_gate_up, m_down, v_down
 ):
@@ -112,39 +261,32 @@
     cot = cotangent.astype(f32)
     grads_in = dispatch([(gates[:, k, None] * cot).astype(bf16) for k in range(topk)])
 
+    hid = w_gate_up.shape[2]
     pre = jnp.einsum("rc,gcf->rgf", inputs, w_gate_up, preferred_element_type=f32)
-    hid = w_gate_up.shape[2]
-    pre = lax.psum_scatter(
-        pre.astype(bf16).reshape(rows, 2 * hid), "dp", scatter_dimension=0, tiled=True
-    ).astype(f32)
+    pre = pre.astype(bf16).reshape(rows, 2 * hid)
     d_hidden = lax.dot_general(
         grads_in, w_down, (((1,), (1,)), ((), ())), preferred_element_type=f32
-    )
-    d_hidden = lax.psum_scatter(
-        d_hidden.astype(bf16), "dp", scatter_dimension=0, tiled=True
-    ).astype(f32)
-    act_in, linear = pre[:, :hid], pre[:, hid:]
-    sig = jax.nn.sigmoid(act_in)
-    hidden = (act_in * sig * linear).astype(bf16)
-    d_act = (d_hidden * linear * sig * (1.0 + act_in * (1.0 - sig))).astype(bf16)
-    d_lin = (d_hidden * act_in * sig).astype(bf16)
-    hidden = lax.all_gather(hidden, "dp", axis=0, tiled=True)
-    d_pre = lax.all_gather(jnp.stack([d_act, d_lin]), "dp", axis=1, tiled=True)
-
-    out_part = jnp.dot(hidden, w_down, preferred_element_type=f32).astype(bf16)
+    ).astype(bf16)
+    acts = line_activations(pre, d_hidden, n_data)
+
+    out_part = jnp.dot(acts[:, :hid], w_down, preferred_element_type=f32).astype(bf16)
     outs = collect(out_part)
     outputs = sum(gates[:, k, None] * outs[k] for k in range(topk)).astype(bf16)
-    in_part = jnp.einsum("grf,gcf->rc", d_pre, w_gate_up, preferred_element_type=f32).astype(bf16)
+    across = (((1,), (1,)), ((), ()))
+    in_part = (
+        lax.dot_general(acts[:, hid : 2 * hid], w_gate_up[0], across, preferred_element_type=f32)
+        + lax.dot_general(acts[:, 2 * hid :], w_gate_up[1], across, preferred_element_type=f32)
+    ).astype(bf16)
     input_grads = sum(collect(in_part)).astype(bf16)
 
     scale = (tok * n_data * n_expert * topk / EXPERTS) ** (-0.5)
     new_wd, new_md, new_vd = (
         x[0]
         for x in grad_adam(
-            hidden, grads_in[None], w_down[None], m_down[None], v_down[None], scale
+            acts, grads_in, 0, w_down[None], m_down[None], v_down[None], scale
         )
     )
-    new_wu, new_mu, new_vu = grad_adam(inputs, d_pre, w_gate_up, m_gate_up, v_gate_up, scale)
+    new_wu, new_mu, new_vu = grad_adam(inputs, acts, 1, w_gate_up, m_gate_up, v_gate_up, scale)
     return (outputs, input_grads, new_wu, new_mu, new_vu, new_wd, new_md, new_vd)
 
 

time: 351 us -> 285 us (0.81)
  blocking collectives: 112 us -> 0 us
  Pallas kernels: 30.5 us -> 134 us
  waiting for transfers between devices: 135 us -> 82.7 us
  between operations: 14 us -> 0.87 us
  starting transfers between devices: 7.59 us -> 18.3 us
  other arithmetic: 6.36 us -> 0.7 us
    all_to_all x2 -> x0, blocking collectives: 112 us -> none  [dispatch(): got = lax.all_to_all(packed, BOTH, split_axis=0, concat_axis=0, tiled=True)]
    all_gather x2 -> x0, waiting for transfers between devices: 105 us -> none  [the longest x1 74.4 us: shards(): d_pre = lax.all_gather(jnp.stack([d_act, d_lin]), 'dp', axis=1, tiled=True)]
    pallas_call x0 -> x1, Pallas kernels: none -> 104 us  [line_activations(): pl.pallas_call(functools.partial(line_body, n, half // count, count), out...]
    all_to_all x0 -> x2, waiting for transfers between devices: none -> 55.9 us  [dispatch(): got = lax.all_to_all(packed, BOTH, split_axis=0, concat_axis=0, tiled=True)]
    reduce_scatter x2 -> x0, waiting for transfers between devices: 29.5 us -> none  [the longest x1 29.5 us: shards(): lax.psum_scatter(d_hidden.astype(bf16), 'dp', scatter_dimension=0, tiled=...]
    all_to_all x2, waiting for transfers between devices: 0.01 us -> 26.8 us  [collect(): back = lax.all_to_all(part, BOTH, split_axis=0, concat_axis=0, tiled=True)]
    all_to_all x0 -> x2, starting transfers between devices: none -> 11 us  [dispatch(): got = lax.all_to_all(packed, BOTH, split_axis=0, concat_axis=0, tiled=True)]
    dot_general x2 -> x3, matrix products: 9.57 us -> 10.6 us  [the longest x1 3.91 us: shards(): lax.dot_general(acts[:, hid:2 * hid], w_gate_up[0], across, preferred_ele...]
  transfers between devices with their start and end apart: 6 -> 4, of which waited for: 3 -> 3; matrix products, arithmetic and copies ran while one was open for 9% -> 8% of each run, Pallas kernels for 9% -> 11%
where the time goes in v2:
time: 285 us; the launch traced here: 284 us
  Pallas kernels  134 us (47%)
  waiting for transfers between devices  82.7 us (29%)
  matrix products  23.9 us (8%)
  local copies, waits for them, and re-layouts  22.5 us (8%)
  starting transfers between devices  18.3 us (6%)
    pallas_call x1, Pallas kernels, line_activations(): pl.pallas_call(functools.partial(line_body, n, half // count, count), out...  104 us
    all_to_all x2, waiting for transfers between devices, dispatch(): got = lax.all_to_all(packed, BOTH, split_axis=0, concat_axis=0, tiled=True)  55.9 us
    pallas_call x2, Pallas kernels, grad_adam(): pl.pallas_call(functools.partial(adam_body, scale), grid=(parts, width //...  30.3 us
    all_to_all x2, waiting for transfers between devices, collect(): back = lax.all_to_all(part, BOTH, split_axis=0, concat_axis=0, tiled=True)  26.8 us
    all_to_all x2, starting transfers between devices, dispatch(): got = lax.all_to_all(packed, BOTH, split_axis=0, concat_axis=0, tiled=True)  11 us
    all_to_all x2, starting transfers between devices, collect(): back = lax.all_to_all(part, BOTH, split_axis=0, concat_axis=0, tiled=True)  7.38 us
    reshape x2, local copies, waits for them, and re-layouts, collect(): part = part.reshape(n_data * n_expert, CAPACITY, block)  5.89 us
  transfers between devices with their start and end apart: 4, of which 3 were waited for; matrix products, arithmetic and copies ran while one was open for 8% of the time, Pallas kernels for 11%

profile of v2, /device:TPU:0, one launch (start us, length us, event | category | flops | bytes accessed | tf_op | source)
XLA Modules:
  0.0 283.5 jit_solution(6106413282324106625)
XLA Ops:
  4.3 7.3 %all-to-all-start = ((bf16[32,20,896]{2,1,0:T(8,128)(2,1)}), bf16[32,20,896]{2,1,0:T(8,128)(2,1)S(1)}, u32[]{:S(2)}, u32[]{:S(2)}) async-start(bf16[32,20,896]{2,1,0:T(8,128)(2,1)} %bitcast.46), calls=%async_computation | async-start | bytes 2752512 | tf_op jit(solution)/shard_map/all_to_all | solution.py:248
  11.6 1.5 convolution_convert_fusion
  15.8 29.4 %all-to-all-done = bf16[32,20,896]{2,1,0:T(8,128)(2,1)S(1)} async-done(((bf16[32,20,896]{2,1,0:T(8,128)(2,1)}), bf16[32,20,896]{2,1,0:T(8,128)(2,1)S(1)}, u32[]{:S(2)}, u32[]{:S(2)}) %all-to-all-start) | async-done | bytes 1146912 | tf_op jit(solution)/shard_map/all_to_all | solution.py:248
  45.2 3.7 %all-to-all-start.1 = ((bf16[32,20,896]{2,1,0:T(8,128)(2,1)}), bf16[32,20,896]{2,1,0:T(8,128)(2,1)}, u32[]{:S(2)}, u32[]{:S(2)}) async-start(bf16[32,20,896]{2,1,0:T(8,128)(2,1)} %bitcast.45), calls=%async_computation.1 | async-start | bytes 2752512 | tf_op jit(solution)/shard_map/all_to_all | solution.py:248
  49.2 5.1 %convert_bitcast_fusion = bf16[2,80,8,1024]{3,2,1,0:T(8,128)(2,1)S(1)} fusion(bf16[640,896,1]{1,0,2:T(8,128)(2,1)S(1)} %reshape.141, bf16[2,896,1024]{2,1,0:T(8,128)(2,1)} %w_ref.1), kind=kOutput, calls=%fused_computation.5 | convolution fusion | flops 2350120960 | bytes 7438336 | tf_op jit(solution)/shard_map/rc,gcf->rgf/dot_general | solution.py:265
  54.3 1.8 copy.27
  56.1 26.4 %all-to-all-done.1 = bf16[32,20,896]{2,1,0:T(8,128)(2,1)} async-done(((bf16[32,20,896]{2,1,0:T(8,128)(2,1)}), bf16[32,20,896]{2,1,0:T(8,128)(2,1)}, u32[]{:S(2)}, u32[]{:S(2)}) %all-to-all-start.1) | async-done | bytes 1146912 | tf_op jit(solution)/shard_map/all_to_all | solution.py:248
  82.5 2.2 reshape.136.b_ref
  84.7 2.6 convolution_convert_fusion.3.g_ref
  87.3 104.2 %line_activations.1.b_ref.a_ref = bf16[640,3072]{1,0:T(8,128)(2,1)} custom-call(bf16[640,2048]{1,0:T(8,128)(2,1)} %bitcast.44, bf16[640,1024]{1,0:T(8,128)(2,1)} %convolution_convert_fusion.3.g_ref), custom_call_target="tpu_custom_call" | custom-call | flops 19660800 | bytes 7864320 | tf_op jit(solution)/shard_map/line_activations/pallas_call | solution.py:208
  191.5 2.9 %fusion.1 = f32[640,896]{1,0:T(8,128)S(1)} fusion(bf16[2,896,1024]{2,1,0:T(8,128)(2,1)S(1)} %copy-done.2, bf16[640,3072]{1,0:T(8,128)(2,1)} %line_activations.1.b_ref.a_ref), kind=kOutput, calls=%fused_computation.7 | convolution fusion | flops 1174405120 | bytes 5439488 | tf_op jit(solution)/shard_map/dot_general | solution.py:278
  194.4 3.9 %add_convert_fusion = bf16[640,896]{1,0:T(8,128)(2,1)} fusion(f32[640,896]{1,0:T(8,128)S(1)} %fusion.1, bf16[2,896,1024]{2,1,0:T(8,128)(2,1)S(1)} %copy-done.2, bf16[640,3072]{1,0:T(8,128)(2,1)} %line_activations.1.b_ref.a_ref), kind=kOutput, calls=%fused_computation.6 | convolution fusion | flops 1175552000 | bytes 6586368 | tf_op jit(solution)/shard_map/dot_general | solution.py:277
  198.3 2.9 %reshape.139 = bf16[32,20,896]{2,1,0:T(8,128)(2,1)} reshape(bf16[640,896]{1,0:T(8,128)(2,1)} %add_convert_fusion) | data formatting | bytes 2293760 | tf_op jit(solution)/shard_map/reshape | solution.py:252
  201.2 3.5 %all-to-all-start.3 = ((bf16[32,20,896]{2,1,0:T(8,128)(2,1)}), bf16[32,20,896]{2,1,0:T(8,128)(2,1)}, u32[]{:S(2)}, u32[]{:S(2)}) async-start(bf16[32,20,896]{2,1,0:T(8,128)(2,1)} %reshape.139), calls=%async_computation.3 | async-start | bytes 2752512 | tf_op jit(solution)/shard_map/all_to_all | solution.py:253
  204.8 3.8 %convolution_convert_fusion.4 = bf16[640,896]{1,0:T(8,128)(2,1)} fusion(bf16[1024,896]{1,0:T(8,128)(2,1)S(1)} %copy-done.4, bf16[640,3072]{1,0:T(8,128)(2,1)} %line_activations.1.b_ref.a_ref), kind=kOutput, calls=%fused_computation.15 | convolution fusion | flops 1174978560 | bytes 4292608 | tf_op jit(solution)/shard_map/dot_general | solution.py:272
  208.6 3.0 %reshape.137 = bf16[32,20,896]{2,1,0:T(8,128)(2,1)} reshape(bf16[640,896]{1,0:T(8,128)(2,1)} %convolution_convert_fusion.4) | data formatting | bytes 2293760 | tf_op jit(solution)/shard_map/reshape | solution.py:252
  211.6 26.8 %all-to-all-done.3 = bf16[32,20,896]{2,1,0:T(8,128)(2,1)} async-done(((bf16[32,20,896]{2,1,0:T(8,128)(2,1)}), bf16[32,20,896]{2,1,0:T(8,128)(2,1)}, u32[]{:S(2)}, u32[]{:S(2)}) %all-to-all-start.3) | async-done | bytes 1146912 | tf_op jit(solution)/shard_map/all_to_all | solution.py:253
  238.4 3.8 %all-to-all-start.2 = ((bf16[32,20,896]{2,1,0:T(8,128)(2,1)}), bf16[32,20,896]{2,1,0:T(8,128)(2,1)}, u32[]{:S(2)}, u32[]{:S(2)}) async-start(bf16[32,20,896]{2,1,0:T(8,128)(2,1)} %reshape.137), calls=%async_computation.2 | async-start | bytes 2752512 | tf_op jit(solution)/shard_map/all_to_all | solution.py:253
  242.2 2.2 reshape.132.a_ref
  244.4 1.5 copy-done.5
  245.9 11.3 %grad_adam.3 = (bf16[1,1024,896]{2,1,0:T(8,128)(2,1)}, f32[1,1024,896]{2,1,0:T(8,128)}, f32[1,1024,896]{2,1,0:T(8,128)}) custom-call(bf16[640,3072]{1,0:T(8,128)(2,1)} %line_activations.1.b_ref.a_ref, bf16[640,896]{1,0:T(8,128)(2,1)S(1)} %reshape.136.b_ref, bf16[1,1024,896]{2,1,0:T(8,128)(2,1)S(1)} %bitcast.43, f32[1,1024,896]{2,1,0:T(8,128)} %bitcast.53, ...), custom_call_target="tpu_custom_call" | custom-call | flops 1174405120 | bytes 18350080 | tf_op jit(solution)/shard_map/grad_adam/pallas_call | solution.py:56
  257.2 19.0 %grad_adam.2 = (bf16[2,896,1024]{2,1,0:T(8,128)(2,1)}, f32[2,896,1024]{2,1,0:T(8,128)}, f32[2,896,1024]{2,1,0:T(8,128)}) custom-call(bf16[640,896]{1,0:T(8,128)(2,1)S(1)} %reshape.132.a_ref, bf16[640,3072]{1,0:T(8,128)(2,1)} %line_activations.1.b_ref.a_ref, bf16[2,896,1024]{2,1,0:T(8,128)(2,1)S(1)} %copy-done.3, f32[2,896,1024]{2,1,0:T(8,128)} %m_ref.1, ...), custom_call_target="tpu_custom_call" | custom-call | flops 2348810240 | bytes 36700160 | tf_op jit(solution)/shard_map/grad_adam/pallas_call | solution.py:56
  276.3 2.2 reshape.140
  279.9 2.2 reshape.138
  (33 shorter events, 9.4 us)
Async XLA Ops:
  0.6 1.7 copy-start
  4.3 7.3 %copy-start.7 = (bf16[128,3584]{1,0:T(8,128)(2,1)S(1)}, bf16[128,3584]{1,0:T(8,128)(2,1)}, u32[]{:S(2)}) copy-start(bf16[128,3584]{1,0:T(8,128)(2,1)} %param.11) | copy-start | bytes 2752516
  4.3 7.3 %copy-start.8 = (f32[128,1]{0,1:T(1,128)S(1)}, f32[128,1]{0,1:T(1,128)}, u32[]{:S(2)}) copy-start(f32[128,1]{0,1:T(1,128)} %param.13) | copy-start | bytes 1540
  4.3 40.9 %all-to-all-start = ((bf16[32,20,896]{2,1,0:T(8,128)(2,1)}), bf16[32,20,896]{2,1,0:T(8,128)(2,1)S(1)}, u32[]{:S(2)}, u32[]{:S(2)}) async-start(bf16[32,20,896]{2,1,0:T(8,128)(2,1)} %bitcast.46), calls=%async_computation | async-start | bytes 2752512 | tf_op jit(solution)/shard_map/all_to_all | solution.py:248
  45.2 4.0 %copy-start.6 = (bf16[32,20,896]{2,1,0:T(8,128)(2,1)}, bf16[32,20,896]{2,1,0:T(8,128)(2,1)S(1)}, u32[]{:S(2)}) copy-start(bf16[32,20,896]{2,1,0:T(8,128)(2,1)S(1)} %all-to-all-done) | copy-start | bytes 3440644
  45.2 37.3 %all-to-all-start.1 = ((bf16[32,20,896]{2,1,0:T(8,128)(2,1)}), bf16[32,20,896]{2,1,0:T(8,128)(2,1)}, u32[]{:S(2)}, u32[]{:S(2)}) async-start(bf16[32,20,896]{2,1,0:T(8,128)(2,1)} %bitcast.45), calls=%async_computation.1 | async-start | bytes 2752512 | tf_op jit(solution)/shard_map/all_to_all | solution.py:248
  56.1 28.6 %copy-start.4 = (bf16[1024,896]{1,0:T(8,128)(2,1)S(1)}, bf16[1024,896]{1,0:T(8,128)(2,1)}, u32[]{:S(2)}) copy-start(bf16[1024,896]{1,0:T(8,128)(2,1)} %param.15) | copy-start | bytes 5505028
  87.3 104.2 %copy-start.2 = (bf16[2,896,1024]{2,1,0:T(8,128)(2,1)S(1)}, bf16[2,896,1024]{2,1,0:T(8,128)(2,1)}, u32[]{:S(2)}) copy-start(bf16[2,896,1024]{2,1,0:T(8,128)(2,1)} %w_ref.1) | copy-start | bytes 11010052
  201.2 37.2 %all-to-all-start.3 = ((bf16[32,20,896]{2,1,0:T(8,128)(2,1)}), bf16[32,20,896]{2,1,0:T(8,128)(2,1)}, u32[]{:S(2)}, u32[]{:S(2)}) async-start(bf16[32,20,896]{2,1,0:T(8,128)(2,1)} %reshape.139), calls=%async_computation.3 | async-start | bytes 2752512 | tf_op jit(solution)/shard_map/all_to_all | solution.py:253
  238.4 41.5 %all-to-all-start.2 = ((bf16[32,20,896]{2,1,0:T(8,128)(2,1)}), bf16[32,20,896]{2,1,0:T(8,128)(2,1)}, u32[]{:S(2)}, u32[]{:S(2)}) async-start(bf16[32,20,896]{2,1,0:T(8,128)(2,1)} %reshape.137), calls=%async_computation.2 | async-start | bytes 2752512 | tf_op jit(solution)/shard_map/all_to_all | solution.py:253
  244.4 1.5 copy-start.5
  245.9 11.3 %copy-start.3 = (bf16[2,896,1024]{2,1,0:T(8,128)(2,1)S(1)}, bf16[2,896,1024]{2,1,0:T(8,128)(2,1)}, u32[]{:S(2)}) copy-start(bf16[2,896,1024]{2,1,0:T(8,128)(2,1)} %w_ref.1) | copy-start | bytes 11010052
  282.1 1.5 copy-start.1

commit v3 on v2

--- a/solution.py
+++ b/solution.py
@@ -27,11 +27,18 @@
     earlier = (jnp.arange(pairs)[:, None] > jnp.arange(pairs)[None, :]).astype(f32)
     before = jnp.dot(earlier, onehot, preferred_element_type=f32)
     slot = jnp.sum(before * onehot, axis=1)
-    at_slot = (slot[:, None] == jnp.arange(CAPACITY, dtype=f32)).astype(f32)
-    sel = onehot[:, :, None, None] * at_slot[:, None, None, :]
-    sel = jnp.broadcast_to(sel, (pairs, EXPERTS, group, CAPACITY))
-    sel = sel.reshape(tok, topk, EXPERTS * group * CAPACITY).astype(bf16)
-    return [sel[:, k] for k in range(topk)]
+    span = 2 * CAPACITY
+    columns = jnp.arange(EXPERTS * group * span, dtype=jnp.int32)
+    expert_of = columns // (group * span)
+    slot_of = (columns % span).astype(f32)
+    mine = routes.reshape(-1)[:, None] == expert_of
+
+    def at(shift):
+        sel = (mine & (slot[:, None] + shift == slot_of)).astype(bf16)
+        return sel.reshape(tok, topk, -1)
+
+    first, second = at(0.0), at(float(CAPACITY))
+    return [(first[:, k], second[:, k]) for k in range(topk)]
 
 
 def adam_body(scale, a_ref, b_ref, w_ref, m_ref, v_ref, nw_ref, nm_ref, nv_ref):
@@ -236,48 +243,55 @@
     topk = routes.shape[1]
     block = width // n_data
     rows = n_data * n_expert * CAPACITY
+    peers = n_data * n_expert
+    span = 2 * CAPACITY
+    hid = w_gate_up.shape[2]
     sels = selections(routes, group)
-
-    def dispatch(per_choice):
-        packed = sum(
-            lax.dot_general(s, r, (((0,), (0,)), ((), ())), preferred_element_type=f32)
-            for s, r in zip(sels, per_choice)
-        ).astype(bf16)
-        packed = packed.reshape(n_expert, CAPACITY, n_data, block).transpose(2, 0, 1, 3)
-        packed = packed.reshape(n_data * n_expert, CAPACITY, block)
-        got = lax.all_to_all(packed, BOTH, split_axis=0, concat_axis=0, tiled=True)
-        return got.reshape(rows, block)
-
-    def collect(part):
-        part = part.reshape(n_data * n_expert, CAPACITY, block)
-        back = lax.all_to_all(part, BOTH, split_axis=0, concat_axis=0, tiled=True)
-        back = back.reshape(n_data, n_expert * CAPACITY, block)
-        return [
-            jnp.einsum("tp,dpc->tdc", s, back, preferred_element_type=f32).reshape(tok, width)
-            for s in sels
-        ]
-
-    inputs = dispatch([tokens] * topk)
+    both = jnp.concatenate([s for pair in sels for s in pair], axis=0)
+
     cot = cotangent.astype(f32)
-    grads_in = dispatch([(gates[:, k, None] * cot).astype(bf16) for k in range(topk)])
-
-    hid = w_gate_up.shape[2]
-    pre = jnp.einsum("rc,gcf->rgf", inputs, w_gate_up, preferred_element_type=f32)
-    pre = pre.astype(bf16).reshape(rows, 2 * hid)
-    d_hidden = lax.dot_general(
-        grads_in, w_down, (((1,), (1,)), ((), ())), preferred_element_type=f32
+    source = []
+    for k in range(topk):
+        source += [tokens, (gates[:, k, None] * cot).astype(bf16)]
+    packed = lax.dot_general(
+        both,
+        jnp.concatenate(source, axis=0),
+        (((0,), (0,)), ((), ())),
+        preferred_element_type=f32,
     ).astype(bf16)
+    packed = jnp.stack([packed[:, d * block : (d + 1) * block] for d in range(n_data)])
+    got = lax.all_to_all(
+        packed.reshape(peers, span, block), BOTH, split_axis=0, concat_axis=0, tiled=True
+    )
+    inputs = got[:, :CAPACITY].reshape(rows, block)
+    grads_in = got[:, CAPACITY:].reshape(rows, block)
+
+    across = (((1,), (1,)), ((), ()))
+    side_by_side = jnp.concatenate([w_gate_up[0], w_gate_up[1]], axis=1)
+    pre = jnp.dot(inputs, side_by_side, preferred_element_type=f32).astype(bf16)
+    d_hidden = lax.dot_general(grads_in, w_down, across, preferred_element_type=f32).astype(bf16)
     acts = line_activations(pre, d_hidden, n_data)
 
     out_part = jnp.dot(acts[:, :hid], w_down, preferred_element_type=f32).astype(bf16)
-    outs = collect(out_part)
-    outputs = sum(gates[:, k, None] * outs[k] for k in range(topk)).astype(bf16)
-    across = (((1,), (1,)), ((), ()))
-    in_part = (
-        lax.dot_general(acts[:, hid : 2 * hid], w_gate_up[0], across, preferred_element_type=f32)
-        + lax.dot_general(acts[:, 2 * hid :], w_gate_up[1], across, preferred_element_type=f32)
+    in_part = lax.dot_general(
+        acts[:, hid:], side_by_side, across, preferred_element_type=f32
     ).astype(bf16)
-    input_grads = sum(collect(in_part)).astype(bf16)
+    parts = jnp.concatenate(
+        [x.reshape(peers, CAPACITY, block) for x in (out_part, in_part)], axis=1
+    )
+    back = lax.all_to_all(parts, BOTH, split_axis=0, concat_axis=0, tiled=True)
+    back = back.reshape(n_data, n_expert * span, block)
+    outputs, input_grads = 0.0, 0.0
+    for k, (first, second) in enumerate(sels):
+        outs, ins = (
+            jnp.concatenate(
+                [jnp.dot(s, back[d], preferred_element_type=f32) for d in range(n_data)], axis=1
+            )
+            for s in (first, second)
+        )
+        outputs = outputs + gates[:, k, None] * outs
+        input_grads = input_grads + ins
+    outputs, input_grads = outputs.astype(bf16), input_grads.astype(bf16)
 
     scale = (tok * n_data * n_expert * topk / EXPERTS) ** (-0.5)
     new_wd, new_md, new_vd = (

time: 285 us -> 267 us (0.937)
  waiting for transfers between devices: 82.7 us -> 70 us
  other arithmetic: 0.7 us -> 9.2 us
  starting transfers between devices: 18.3 us -> 11.9 us
  local copies, waits for them, and re-layouts: 22.5 us -> 18.2 us
    all_to_all x4 -> x2, waiting for transfers between devices: 82.7 us -> 70 us  [the longest x1 48.9 us: shards(): lax.all_to_all(packed.reshape(peers, span, block), BOTH, split_axis=0, co...]
    reshape x10 -> x4, local copies, waits for them, and re-layouts: 18.3 us -> 8.47 us  [the longest x2 4.13 us: shards(): x.reshape(peers, CAPACITY, block)]
    all_to_all x4 -> x2, starting transfers between devices: 18.3 us -> 11.9 us  [the longest x1 7.3 us: shards(): lax.all_to_all(packed.reshape(peers, span, block), BOTH, split_axis=0, co...]
    concatenate x0 -> x2, other arithmetic: none -> 4.81 us  [the longest x1 3.82 us: shards(): jnp.concatenate([x.reshape(peers, CAPACITY, block) for x in (out_part, in...]
    squeeze x0 -> x1, local copies, waits for them, and re-layouts: none -> 4.26 us  [shards(): side_by_side = jnp.concatenate([w_gate_up[0], w_gate_up[1]], axis=1)]
    slice x0 -> x2, local copies, waits for them, and re-layouts: none -> 3.72 us  [the longest x1 1.96 us: shards(): grads_in = got[:, CAPACITY:].reshape(rows, block)]
    dot_general x8 -> x12, matrix products: 19.2 us -> 16.9 us  [the longest x1 4.77 us: shards(): lax.dot_general(acts[:, hid:], side_by_side, across, preferred_element_ty...]
  transfers between devices with their start and end apart: 4 -> 2, of which waited for: 3 -> 2; matrix products, arithmetic and copies ran while one was open for 8% -> 2% of each run, Pallas kernels for 11% -> 11%
where the time goes in v3:
time: 267 us; the launch traced here: 266 us
  Pallas kernels  134 us (50%)
  waiting for transfers between devices  70 us (26%)
  matrix products  21.7 us (8%)
  local copies, waits for them, and re-layouts  18.2 us (7%)
  starting transfers between devices  11.9 us (4%)
  other arithmetic  9.2 us (3%)
    pallas_call x1, Pallas kernels, line_activations(): pl.pallas_call(functools.partial(line_body, n, half // count, count), out...  103 us
    all_to_all x1, waiting for transfers between devices, shards(): lax.all_to_all(packed.reshape(peers, span, block), BOTH, split_axis=0, co...  48.9 us
    pallas_call x2, Pallas kernels, grad_adam(): pl.pallas_call(functools.partial(adam_body, scale), grid=(parts, width //...  30.3 us
    all_to_all x1, waiting for transfers between devices, shards(): back = lax.all_to_all(parts, BOTH, split_axis=0, concat_axis=0, tiled=True)  21.1 us
    all_to_all x1, starting transfers between devices, shards(): lax.all_to_all(packed.reshape(peers, span, block), BOTH, split_axis=0, co...  7.3 us
  transfers between devices with their start and end apart: 2, of which 2 were waited for; matrix products, arithmetic and copies ran while one was open for 2% of the time, Pallas kernels for 11%

profile of v3, /device:TPU:0, one launch (start us, length us, event | category | flops | bytes accessed | tf_op | source)
XLA Modules:
  0.0 265.6 jit_solution(14858667188365635155)
XLA Ops:
  1.6 1.4 multiply_convert_fusion
  4.2 1.7 pad_maximum_fusion.3
  5.9 7.3 %all-to-all-start = ((bf16[32,40,896]{2,1,0:T(8,128)(2,1)}), bf16[32,40,896]{2,1,0:T(8,128)(2,1)S(1)}, u32[]{:S(2)}, u32[]{:S(2)}) async-start(bf16[32,40,896]{2,1,0:T(8,128)(2,1)} %bitcast.38), calls=%async_computation | async-start | bytes 4587520 | tf_op jit(solution)/shard_map/all_to_all | solution.py:263
  13.2 4.3 %slice_bitcast_fusion.1 = (bf16[896,1024]{1,0:T(8,128)(2,1)}, bf16[896,1024]{1,0:T(8,128)(2,1)}) fusion(bf16[2,896,1024]{2,1,0:T(8,128)(2,1)} %w_ref.1), kind=kLoop, calls=%fused_computation.13 | loop fusion | bytes 7340032 | tf_op jit(solution)/shard_map/squeeze | solution.py:270
  17.5 48.9 %all-to-all-done = bf16[32,40,896]{2,1,0:T(8,128)(2,1)S(1)} async-done(((bf16[32,40,896]{2,1,0:T(8,128)(2,1)}), bf16[32,40,896]{2,1,0:T(8,128)(2,1)S(1)}, u32[]{:S(2)}, u32[]{:S(2)}) %all-to-all-start) | async-done | bytes 2293792 | tf_op jit(solution)/shard_map/all_to_all | solution.py:263
  66.4 2.0 fusion.32
  68.3 2.2 reshape.67.b_ref
  70.5 2.2 reshape.66.a_ref
  72.7 4.3 %convolution_convert_fusion.2.g_ref = bf16[640,1024]{1,0:T(8,128)(2,1)} fusion(bf16[640,896]{1,0:T(8,128)(2,1)S(1)} %reshape.67.b_ref, bf16[1024,896]{1,0:T(8,128)(2,1)} %param.15), kind=kOutput, calls=%fused_computation.15 | convolution fusion | flops 1175060480 | bytes 4292608 | tf_op jit(solution)/shard_map/dot_general | solution.py:272
  77.0 4.3 %convolution_convert_fusion.1.ab_ref = bf16[640,2048]{1,0:T(8,128)(2,1)} fusion(bf16[640,896]{1,0:T(8,128)(2,1)S(1)} %reshape.66.a_ref, bf16[896,1024]{1,0:T(8,128)(2,1)S(1)} %copy-done.4, bf16[896,1024]{1,0:T(8,128)(2,1)S(1)} %copy-done.3), kind=kOutput, calls=%fused_computation.2 | convolution fusion | flops 2357460992 | bytes 7438336 | tf_op jit(solution)/shard_map/dot_general | solution.py:271
  81.2 103.4 %line_activations.1.b_ref.a_ref = bf16[640,3072]{1,0:T(8,128)(2,1)} custom-call(bf16[640,2048]{1,0:T(8,128)(2,1)} %convolution_convert_fusion.1.ab_ref, bf16[640,1024]{1,0:T(8,128)(2,1)} %convolution_convert_fusion.2.g_ref), custom_call_target="tpu_custom_call" | custom-call | flops 19660800 | bytes 7864320 | tf_op jit(solution)/shard_map/line_activations/pallas_call | solution.py:215
  184.6 4.8 %fusion.6 = bf16[640,896]{1,0:T(8,128)(2,1)S(1)} fusion(bf16[896,1024]{1,0:T(8,128)(2,1)S(1)} %copy-done.4, bf16[896,1024]{1,0:T(8,128)(2,1)S(1)} %copy-done.3, bf16[640,3072]{1,0:T(8,128)(2,1)} %line_activations.1.b_ref.a_ref), kind=kOutput, calls=%fused_computation.17 | convolution fusion | flops 2356723712 | bytes 7438336 | tf_op jit(solution)/shard_map/dot_general | solution.py:276
  189.4 3.9 %convolution_convert_fusion.3 = bf16[640,896]{1,0:T(8,128)(2,1)} fusion(bf16[1024,896]{1,0:T(8,128)(2,1)S(1)} %copy-done.1, bf16[640,3072]{1,0:T(8,128)(2,1)} %line_activations.1.b_ref.a_ref), kind=kOutput, calls=%fused_computation.16 | convolution fusion | flops 1174978560 | bytes 4292608 | tf_op jit(solution)/shard_map/dot_general | solution.py:275
  193.3 1.2 reshape.69
  194.5 2.9 %reshape.68 = bf16[32,20,896]{2,1,0:T(8,128)(2,1)} reshape(bf16[640,896]{1,0:T(8,128)(2,1)} %convolution_convert_fusion.3) | data formatting | bytes 2293760 | tf_op jit(solution)/shard_map/reshape | solution.py:280
  197.4 3.8 %pad_maximum_fusion.4 = bf16[32,40,896]{2,1,0:T(8,128)(2,1)} fusion(bf16[32,20,896]{2,1,0:T(8,128)(2,1)} %reshape.69, bf16[32,20,896]{2,1,0:T(8,128)(2,1)} %reshape.68), kind=kLoop, calls=%fused_computation.6 | loop fusion | flops 4587520 | bytes 4587520 | tf_op jit(solution)/shard_map/concatenate | solution.py:279
  201.2 4.6 %all-to-all-start.1 = ((bf16[32,40,896]{2,1,0:T(8,128)(2,1)}), bf16[32,40,896]{2,1,0:T(8,128)(2,1)}, u32[]{:S(2)}, u32[]{:S(2)}) async-start(bf16[32,40,896]{2,1,0:T(8,128)(2,1)} %pad_maximum_fusion.4), calls=%async_computation.1 | async-start | bytes 4587520 | tf_op jit(solution)/shard_map/all_to_all | solution.py:282
  205.9 1.5 copy-done.2
  207.4 11.3 %grad_adam.3 = (bf16[1,1024,896]{2,1,0:T(8,128)(2,1)}, f32[1,1024,896]{2,1,0:T(8,128)}, f32[1,1024,896]{2,1,0:T(8,128)}) custom-call(bf16[640,3072]{1,0:T(8,128)(2,1)} %line_activations.1.b_ref.a_ref, bf16[640,896]{1,0:T(8,128)(2,1)S(1)} %reshape.67.b_ref, bf16[1,1024,896]{2,1,0:T(8,128)(2,1)S(1)} %bitcast.37, f32[1,1024,896]{2,1,0:T(8,128)} %bitcast.47, ...), custom_call_target="tpu_custom_call" | custom-call | flops 1174405120 | bytes 18350080 | tf_op jit(solution)/shard_map/grad_adam/pallas_call | solution.py:63
  218.7 19.0 %grad_adam.2 = (bf16[2,896,1024]{2,1,0:T(8,128)(2,1)}, f32[2,896,1024]{2,1,0:T(8,128)}, f32[2,896,1024]{2,1,0:T(8,128)}) custom-call(bf16[640,896]{1,0:T(8,128)(2,1)S(1)} %reshape.66.a_ref, bf16[640,3072]{1,0:T(8,128)(2,1)} %line_activations.1.b_ref.a_ref, bf16[2,896,1024]{2,1,0:T(8,128)(2,1)S(1)} %copy-done, f32[2,896,1024]{2,1,0:T(8,128)} %m_ref.1, ...), custom_call_target="tpu_custom_call" | custom-call | flops 2348810240 | bytes 36700160 | tf_op jit(solution)/shard_map/grad_adam/pallas_call | solution.py:63
  237.7 21.1 %all-to-all-done.1 = bf16[32,40,896]{2,1,0:T(8,128)(2,1)} async-done(((bf16[32,40,896]{2,1,0:T(8,128)(2,1)}), bf16[32,40,896]{2,1,0:T(8,128)(2,1)}, u32[]{:S(2)}, u32[]{:S(2)}) %all-to-all-start.1) | async-done | bytes 2293792 | tf_op jit(solution)/shard_map/all_to_all | solution.py:282
  258.9 1.8 fusion.31
  263.5 1.1 fusion.5
  264.6 1.0 pad_maximum_fusion.7
  (29 shorter events, 4.9 us)
Async XLA Ops:
  0.6 2.4 copy-start.5
  0.6 2.5 copy-start.7
  5.9 60.4 %all-to-all-start = ((bf16[32,40,896]{2,1,0:T(8,128)(2,1)}), bf16[32,40,896]{2,1,0:T(8,128)(2,1)S(1)}, u32[]{:S(2)}, u32[]{:S(2)}) async-start(bf16[32,40,896]{2,1,0:T(8,128)(2,1)} %bitcast.38), calls=%async_computation | async-start | bytes 4587520 | tf_op jit(solution)/shard_map/all_to_all | solution.py:263
  72.7 4.3 %copy-start.3 = (bf16[896,1024]{1,0:T(8,128)(2,1)S(1)}, bf16[896,1024]{1,0:T(8,128)(2,1)}, u32[]{:S(2)}) copy-start(bf16[896,1024]{1,0:T(8,128)(2,1)} %get-tuple-element.20) | copy-start | bytes 5505028
  72.7 4.3 %copy-start.4 = (bf16[896,1024]{1,0:T(8,128)(2,1)S(1)}, bf16[896,1024]{1,0:T(8,128)(2,1)}, u32[]{:S(2)}) copy-start(bf16[896,1024]{1,0:T(8,128)(2,1)} %get-tuple-element.21) | copy-start | bytes 5505028
  184.6 4.8 %copy-start.1 = (bf16[1024,896]{1,0:T(8,128)(2,1)S(1)}, bf16[1024,896]{1,0:T(8,128)(2,1)}, u32[]{:S(2)}) copy-start(bf16[1024,896]{1,0:T(8,128)(2,1)} %param.15) | copy-start | bytes 5505028
  201.2 57.6 %all-to-all-start.1 = ((bf16[32,40,896]{2,1,0:T(8,128)(2,1)}), bf16[32,40,896]{2,1,0:T(8,128)(2,1)}, u32[]{:S(2)}, u32[]{:S(2)}) async-start(bf16[32,40,896]{2,1,0:T(8,128)(2,1)} %pad_maximum_fusion.4), calls=%async_computation.1 | async-start | bytes 4587520 | tf_op jit(solution)/shard_map/all_to_all | solution.py:282
  205.9 1.5 copy-start.2
  207.4 11.3 %copy-start = (bf16[2,896,1024]{2,1,0:T(8,128)(2,1)S(1)}, bf16[2,896,1024]{2,1,0:T(8,128)(2,1)}, u32[]{:S(2)}) copy-start(bf16[2,896,1024]{2,1,0:T(8,128)(2,1)} %w_ref.1) | copy-start | bytes 11010052
  262.1 1.5 copy-start.6

commit v4 on v3

--- a/solution.py
+++ b/solution.py
@@ -9,6 +9,7 @@
 
 EXPERTS = 8
 CAPACITY = 20
+MAIN = 16
 BOTH = ("dp", "expert")
 
 first_decay = 0.9
@@ -33,11 +34,11 @@
     slot_of = (columns % span).astype(f32)
     mine = routes.reshape(-1)[:, None] == expert_of
 
-    def at(shift):
-        sel = (mine & (slot[:, None] + shift == slot_of)).astype(bf16)
-        return sel.reshape(tok, topk, -1)
-
-    first, second = at(0.0), at(float(CAPACITY))
+    def at(place):
+        return (mine & (place[:, None] == slot_of)).astype(bf16).reshape(tok, topk, -1)
+
+    first = at(jnp.where(slot < MAIN, slot, slot + MAIN))
+    second = at(jnp.where(slot < MAIN, slot + MAIN, slot + CAPACITY))
     return [(first[:, k], second[:, k]) for k in range(topk)]
 
 
@@ -55,7 +56,7 @@
 
 
 def grad_adam(a, b, first, w, m, v, scale):
-    rows = a.shape[0]
+    rows = a.shape[1]
     parts, width, cols = w.shape
     tile = 128 if width % 128 == 0 else width
     state = pl.BlockSpec((None, tile, cols), lambda g, i: (g, i, 0))
@@ -64,8 +65,8 @@
         functools.partial(adam_body, scale),
         grid=(parts, width // tile),
         in_specs=[
-            pl.BlockSpec((rows, tile), lambda g, i: (0, i)),
-            pl.BlockSpec((rows, cols), lambda g, i: (0, first + g)),
+            pl.BlockSpec((None, rows, tile), lambda g, i: (0, 0, i)),
+            pl.BlockSpec((None, rows, cols), lambda g, i: (first + g, 0, 0)),
             state,
             state,
             state,
@@ -87,11 +88,12 @@
 SKEW = 2
 
 
-def line_body(n, chunk, count, ab_ref, g_ref, out_ref, sums, got, send, recv):
+def line_body(n, chunk, count, splits, ab_ref, g_ref, out_ref, sums, got, send, recv):
     d = lax.axis_index("dp")
     last = n - 1
     hid = g_ref.shape[1]
-    half = chunk * count
+    half = chunk * (count // splits)
+    width = hid // splits
     has_low, has_high = d > 0, d < last
 
     barrier = pltpu.get_barrier_semaphore()
@@ -110,12 +112,23 @@
     ends = (d == last, d == 0)
 
     def rows_of(w, c):
-        return pl.ds(pl.multiple_of(w * half + c * chunk, 16), chunk)
+        return pl.ds(pl.multiple_of(w * half + lax.div(c, splits) * chunk, 16), chunk)
+
+    def columns_of(c, part):
+        start = part * hid + lax.rem(c, splits) * width
+        return pl.ds(pl.multiple_of(start, 128), width)
+
+    def piece(w, c):
+        return (slice(None), rows_of(w, c), columns_of(c, 0))
+
+    def own(w, c, part):
+        ref = g_ref if part == 2 else ab_ref
+        return ref[rows_of(w, c), columns_of(c, part if part < 2 else 0)]
 
     def sum_copy(w, c):
         return pltpu.make_async_remote_copy(
-            src_ref=sums.at[rows_of(w, c), :],
-            dst_ref=got.at[rows_of(w, c), :],
+            src_ref=sums.at[piece(w, c)],
+            dst_ref=got.at[piece(w, c)],
             send_sem=send.at[w, c],
             recv_sem=recv.at[w, c],
             device_id={"dp": peers[w]},
@@ -124,8 +137,8 @@
 
     def result_copy(w, c):
         return pltpu.make_async_remote_copy(
-            src_ref=out_ref.at[rows_of(w, c), :],
-            dst_ref=out_ref.at[rows_of(w, c), :],
+            src_ref=out_ref.at[piece(w, c)],
+            dst_ref=out_ref.at[piece(w, c)],
             send_sem=send.at[2 + w, c],
             recv_sem=recv.at[2 + w, c],
             device_id={"dp": peers[1 - w]},
@@ -139,12 +152,12 @@
 
             @pl.when((c >= 0) & (c < count))
             def _():
-                rows = rows_of(w, c)
+                rows, columns = rows_of(w, c), columns_of(c, 0)
 
                 @pl.when(starts[w])
                 def _():
-                    sums[rows, : 2 * hid] = ab_ref[rows, :]
-                    sums[rows, 2 * hid :] = g_ref[rows, :]
+                    for part in range(3):
+                        sums[part, rows, columns] = own(w, c, part)
                     sum_copy(w, c).start()
 
                 @pl.when(jnp.logical_not(starts[w]))
@@ -153,25 +166,22 @@
 
                 @pl.when(jnp.logical_not(starts[w] | ends[w]))
                 def _():
-                    sums[rows, : 2 * hid] = (
-                        got[rows, : 2 * hid].astype(f32) + ab_ref[rows, :].astype(f32)
-                    ).astype(bf16)
-                    sums[rows, 2 * hid :] = (
-                        got[rows, 2 * hid :].astype(f32) + g_ref[rows, :].astype(f32)
-                    ).astype(bf16)
+                    for part in range(3):
+                        sums[part, rows, columns] = (
+                            got[part, rows, columns].astype(f32) + own(w, c, part).astype(f32)
+                        ).astype(bf16)
                     sum_copy(w, c).start()
 
                 @pl.when(ends[w])
                 def _():
-                    a = got[rows, :hid].astype(f32) + ab_ref[rows, :hid].astype(f32)
-                    b = got[rows, hid : 2 * hid].astype(f32) + ab_ref[rows, hid:].astype(f32)
-                    g = got[rows, 2 * hid :].astype(f32) + g_ref[rows, :].astype(f32)
+                    a, b, g = (
+                        got[part, rows, columns].astype(f32) + own(w, c, part).astype(f32)
+                        for part in range(3)
+                    )
                     sig = jax.nn.sigmoid(a)
-                    out_ref[rows, :hid] = (a * sig * b).astype(bf16)
-                    out_ref[rows, hid : 2 * hid] = (
-                        g * b * sig * (1.0 + a * (1.0 - sig))
-                    ).astype(bf16)
-                    out_ref[rows, 2 * hid :] = (g * a * sig).astype(bf16)
+                    out_ref[0, rows, columns] = (a * sig * b).astype(bf16)
+                    out_ref[1, rows, columns] = (g * b * sig * (1.0 + a * (1.0 - sig))).astype(bf16)
+                    out_ref[2, rows, columns] = (g * a * sig).astype(bf16)
                     result_copy(w, c).start()
 
         for w in range(2):
@@ -210,10 +220,13 @@
     rows, hid = g.shape
     half = rows // 2
     count = max(c for c in range(1, 21) if half % (16 * c) == 0)
+    chunk = half // count
+    splits = 2 if hid % 256 == 0 else 1
+    count = count * splits
     whole = pl.BlockSpec(memory_space=pltpu.VMEM)
-    full = jax.ShapeDtypeStruct((rows, 3 * hid), bf16)
+    full = jax.ShapeDtypeStruct((3, rows, hid), bf16)
     return pl.pallas_call(
-        functools.partial(line_body, n, half // count, count),
+        functools.partial(line_body, n, chunk, count, splits),
         out_shape=full,
         in_specs=[whole, whole],
         out_specs=whole,
@@ -242,10 +255,8 @@
     tok, width = tokens.shape
     topk = routes.shape[1]
     block = width // n_data
-    rows = n_data * n_expert * CAPACITY
     peers = n_data * n_expert
     span = 2 * CAPACITY
-    hid = w_gate_up.shape[2]
     sels = selections(routes, group)
     both = jnp.concatenate([s for pair in sels for s in pair], axis=0)
 
@@ -263,8 +274,13 @@
     got = lax.all_to_all(
         packed.reshape(peers, span, block), BOTH, split_axis=0, concat_axis=0, tiled=True
     )
-    inputs = got[:, :CAPACITY].reshape(rows, block)
-    grads_in = got[:, CAPACITY:].reshape(rows, block)
+
+    def joined(main, other):
+        return jnp.concatenate([main.reshape(-1, block), other.reshape(-1, block)], axis=0)
+
+    rest = CAPACITY - MAIN
+    inputs = joined(got[:, :MAIN], got[:, 2 * MAIN : 2 * MAIN + rest])
+    grads_in = joined(got[:, MAIN : 2 * MAIN], got[:, 2 * MAIN + rest :])
 
     across = (((1,), (1,)), ((), ()))
     side_by_side = jnp.concatenate([w_gate_up[0], w_gate_up[1]], axis=1)
@@ -272,12 +288,17 @@
     d_hidden = lax.dot_general(grads_in, w_down, across, preferred_element_type=f32).astype(bf16)
     acts = line_activations(pre, d_hidden, n_data)
 
-    out_part = jnp.dot(acts[:, :hid], w_down, preferred_element_type=f32).astype(bf16)
+    out_part = jnp.dot(acts[0], w_down, preferred_element_type=f32).astype(bf16)
     in_part = lax.dot_general(
-        acts[:, hid:], side_by_side, across, preferred_element_type=f32
+        jnp.concatenate([acts[1], acts[2]], axis=1),
+        side_by_side,
+        across,
+        preferred_element_type=f32,
     ).astype(bf16)
     parts = jnp.concatenate(
-        [x.reshape(peers, CAPACITY, block) for x in (out_part, in_part)], axis=1
+        [x[: peers * MAIN].reshape(peers, MAIN, block) for x in (out_part, in_part)]
+        + [x[peers * MAIN :].reshape(peers, rest, block) for x in (out_part, in_part)],
+        axis=1,
     )
     back = lax.all_to_all(parts, BOTH, split_axis=0, concat_axis=0, tiled=True)
     back = back.reshape(n_data, n_expert * span, block)
@@ -297,10 +318,10 @@
     new_wd, new_md, new_vd = (
         x[0]
         for x in grad_adam(
-            acts, grads_in, 0, w_down[None], m_down[None], v_down[None], scale
+            acts, grads_in[None], 0, w_down[None], m_down[None], v_down[None], scale
         )
     )
-    new_wu, new_mu, new_vu = grad_adam(inputs, acts, 1, w_gate_up, m_gate_up, v_gate_up, scale)
+    new_wu, new_mu, new_vu = grad_adam(inputs[None], acts, 1, w_gate_up, m_gate_up, v_gate_up, scale)
     return (outputs, input_grads, new_wu, new_mu, new_vu, new_wd, new_md, new_vd)
 
 

time: 267 us -> 265 us (level)
  local copies, waits for them, and re-layouts: 18.2 us -> 14.4 us
  matrix products: 21.7 us -> 18.5 us
  Pallas kernels: 134 us -> 137 us
    reshape x4, local copies, waits for them, and re-layouts: 8.47 us -> 1.86 us  [the longest x2 1.74 us: shards(): x[peers * MAIN:].reshape(peers, rest, block)]
    pallas_call x1, Pallas kernels: 103 us -> 106 us  [line_activations(): pl.pallas_call(functools.partial(line_body, n, chunk, count, splits), out...]
    dot_general x2, matrix products: 8.63 us -> 5.9 us  [the longest x1 2.98 us: shards(): out_part = jnp.dot(acts[0], w_down, preferred_element_type=f32).astype(bf16)]
  transfers between devices with their start and end apart: 2 -> 2, of which waited for: 2 -> 2; matrix products, arithmetic and copies ran while one was open for 2% -> 2% of each run, Pallas kernels for 11% -> 12%
where the time goes in v4:
time: 265 us; the launch traced here: 264 us
  Pallas kernels  137 us (52%)
  waiting for transfers between devices  70.1 us (26%)
  matrix products  18.5 us (7%)
  local copies, waits for them, and re-layouts  14.4 us (5%)
  starting transfers between devices  12.8 us (5%)
  other arithmetic  10.8 us (4%)
    pallas_call x1, Pallas kernels, line_activations(): pl.pallas_call(functools.partial(line_body, n, chunk, count, splits), out...  106 us
    all_to_all x1, waiting for transfers between devices, shards(): lax.all_to_all(packed.reshape(peers, span, block), BOTH, split_axis=0, co...  48.9 us
    pallas_call x2, Pallas kernels, grad_adam(): pl.pallas_call(functools.partial(adam_body, scale), grid=(parts, width //...  30.4 us
    all_to_all x1, waiting for transfers between devices, shards(): back = lax.all_to_all(parts, BOTH, split_axis=0, concat_axis=0, tiled=True)  21.2 us
    all_to_all x1, starting transfers between devices, shards(): lax.all_to_all(packed.reshape(peers, span, block), BOTH, split_axis=0, co...  7.3 us
    all_to_all x1, starting transfers between devices, shards(): back = lax.all_to_all(parts, BOTH, split_axis=0, concat_axis=0, tiled=True)  5.49 us
  transfers between devices with their start and end apart: 2, of which 2 were waited for; matrix products, arithmetic and copies ran while one was open for 2% of the time, Pallas kernels for 12%

profile of v4, /device:TPU:0, one launch (start us, length us, event | category | flops | bytes accessed | tf_op | source)
XLA Modules:
  0.0 263.9 jit_solution(11978264570516077996)
XLA Ops:
  1.5 1.4 multiply_convert_fusion
  3.8 2.0 convolution_convert_fusion
  6.0 1.7 pad_maximum_fusion.3
  7.7 7.3 %all-to-all-start = ((bf16[32,40,896]{2,1,0:T(8,128)(2,1)}), bf16[32,40,896]{2,1,0:T(8,128)(2,1)S(1)}, u32[]{:S(2)}, u32[]{:S(2)}) async-start(bf16[32,40,896]{2,1,0:T(8,128)(2,1)} %bitcast.51), calls=%async_computation | async-start | bytes 4587520 | tf_op jit(solution)/shard_map/all_to_all | solution.py:274
  15.0 4.3 %slice_bitcast_fusion.1 = (bf16[896,1024]{1,0:T(8,128)(2,1)}, bf16[896,1024]{1,0:T(8,128)(2,1)}) fusion(bf16[2,896,1024]{2,1,0:T(8,128)(2,1)} %w_ref.1), kind=kLoop, calls=%fused_computation.15 | loop fusion | bytes 7340032 | tf_op jit(solution)/shard_map/squeeze | solution.py:286
  19.2 48.9 %all-to-all-done = bf16[32,40,896]{2,1,0:T(8,128)(2,1)S(1)} async-done(((bf16[32,40,896]{2,1,0:T(8,128)(2,1)}), bf16[32,40,896]{2,1,0:T(8,128)(2,1)S(1)}, u32[]{:S(2)}, u32[]{:S(2)}) %all-to-all-start) | async-done | bytes 2293792 | tf_op jit(solution)/shard_map/all_to_all | solution.py:274
  68.3 1.2 copy-done.3
  69.6 1.7 fusion.38
  71.6 2.6 convolution_convert_fusion.2.g_ref
  74.2 4.3 %convolution_convert_fusion.1.ab_ref = bf16[640,2048]{1,0:T(8,128)(2,1)} fusion(bf16[896,1024]{1,0:T(8,128)(2,1)S(1)} %copy-done.6, bf16[896,1024]{1,0:T(8,128)(2,1)S(1)} %copy-done.5, bf16[128,896]{1,0:T(8,128)(2,1)S(1)} %reshape.83, bf16[512,896]{1,0:T(8,128)(2,1)S(1)} %bitcast.60), kind=kOutput, calls=%fused_computation.2 | convolution fusion | flops 2359754752 | bytes 7438336 | tf_op jit(solution)/shard_map/dot_general | solution.py:287
  78.5 106.2 %line_activations.1.b_ref.a_ref = bf16[3,640,1024]{2,1,0:T(8,128)(2,1)} custom-call(bf16[640,2048]{1,0:T(8,128)(2,1)} %convolution_convert_fusion.1.ab_ref, bf16[640,1024]{1,0:T(8,128)(2,1)} %convolution_convert_fusion.2.g_ref), custom_call_target="tpu_custom_call" | custom-call | flops 19660800 | bytes 7864320 | tf_op jit(solution)/shard_map/line_activations/pallas_call | solution.py:228
  184.7 3.0 %convolution_convert_fusion.3 = bf16[640,896]{1,0:T(8,128)(2,1)S(1)} fusion(bf16[1024,896]{1,0:T(8,128)(2,1)S(1)} %copy-done.1, bf16[3,640,1024]{2,1,0:T(8,128)(2,1)} %line_activations.1.b_ref.a_ref), kind=kOutput, calls=%fused_computation.19 | convolution fusion | flops 1174978560 | bytes 4292608 | tf_op jit(solution)/shard_map/dot_general | solution.py:291
  187.7 1.0 slice.100
  188.9 2.9 %fusion.8 = bf16[640,896]{1,0:T(8,128)(2,1)S(1)} fusion(bf16[896,1024]{1,0:T(8,128)(2,1)S(1)} %copy-done.6, bf16[896,1024]{1,0:T(8,128)(2,1)S(1)} %copy-done.5, bf16[640,1024]{1,0:T(8,128)(2,1)S(1)} %get-tuple-element.21, bf16[640,1024]{1,0:T(8,128)(2,1)S(1)} %get-tuple-element.20), kind=kOutput, calls=%fused_computation.18 | convolution fusion | flops 2361966592 | bytes 7438336 | tf_op jit(solution)/shard_map/dot_general | solution.py:292
  192.6 1.0 slice.101
  194.3 1.0 reshape.89
  195.3 3.4 %pad_maximum_fusion.4 = bf16[32,40,896]{2,1,0:T(8,128)(2,1)} fusion(bf16[32,4,896]{2,1,0:T(4,128)(2,1)S(1)} %reshape.89, bf16[32,4,896]{2,1,0:T(4,128)(2,1)} %reshape.88, bf16[32,16,896]{2,1,0:T(8,128)(2,1)} %bitcast.67, bf16[32,16,896]{2,1,0:T(8,128)(2,1)} %bitcast.66), kind=kLoop, calls=%fused_computation.8 | loop fusion | flops 9175040 | bytes 4587520 | tf_op jit(solution)/shard_map/concatenate | solution.py:298
  198.7 5.5 %all-to-all-start.1 = ((bf16[32,40,896]{2,1,0:T(8,128)(2,1)}), bf16[32,40,896]{2,1,0:T(8,128)(2,1)}, u32[]{:S(2)}, u32[]{:S(2)}) async-start(bf16[32,40,896]{2,1,0:T(8,128)(2,1)} %pad_maximum_fusion.4), calls=%async_computation.1 | async-start | bytes 4587520 | tf_op jit(solution)/shard_map/all_to_all | solution.py:303
  204.2 1.3 fusion.14.b_ref
  205.4 11.3 %grad_adam.3 = (bf16[1,1024,896]{2,1,0:T(8,128)(2,1)}, f32[1,1024,896]{2,1,0:T(8,128)}, f32[1,1024,896]{2,1,0:T(8,128)}) custom-call(bf16[3,640,1024]{2,1,0:T(8,128)(2,1)} %line_activations.1.b_ref.a_ref, bf16[1,640,896]{2,1,0:T(8,128)(2,1)S(1)} %fusion.14.b_ref, bf16[1,1024,896]{2,1,0:T(8,128)(2,1)S(1)} %bitcast.50, f32[1,1024,896]{2,1,0:T(8,128)} %bitcast.64, ...), custom_call_target="tpu_custom_call" | custom-call | flops 1174405120 | bytes 18350080 | tf_op jit(solution)/shard_map/grad_adam/pallas_call | solution.py:64
  216.9 19.0 %grad_adam.2 = (bf16[2,896,1024]{2,1,0:T(8,128)(2,1)}, f32[2,896,1024]{2,1,0:T(8,128)}, f32[2,896,1024]{2,1,0:T(8,128)}) custom-call(bf16[1,640,896]{2,1,0:T(8,128)(2,1)S(1)} %fusion.15.a_ref, bf16[3,640,1024]{2,1,0:T(8,128)(2,1)} %line_activations.1.b_ref.a_ref, bf16[2,896,1024]{2,1,0:T(8,128)(2,1)S(1)} %copy-done, f32[2,896,1024]{2,1,0:T(8,128)} %m_ref.1, ...), custom_call_target="tpu_custom_call" | custom-call | flops 2348810240 | bytes 36700160 | tf_op jit(solution)/shard_map/grad_adam/pallas_call | solution.py:64
  235.9 21.2 %all-to-all-done.1 = bf16[32,40,896]{2,1,0:T(8,128)(2,1)} async-done(((bf16[32,40,896]{2,1,0:T(8,128)(2,1)}), bf16[32,40,896]{2,1,0:T(8,128)(2,1)}, u32[]{:S(2)}, u32[]{:S(2)}) %all-to-all-start.1) | async-done | bytes 2293792 | tf_op jit(solution)/shard_map/all_to_all | solution.py:303
  257.2 1.8 fusion.37
  261.8 1.1 fusion.7
  (39 shorter events, 8.0 us)
Async XLA Ops:
  7.7 60.4 %all-to-all-start = ((bf16[32,40,896]{2,1,0:T(8,128)(2,1)}), bf16[32,40,896]{2,1,0:T(8,128)(2,1)S(1)}, u32[]{:S(2)}, u32[]{:S(2)}) async-start(bf16[32,40,896]{2,1,0:T(8,128)(2,1)} %bitcast.51), calls=%async_computation | async-start | bytes 4587520 | tf_op jit(solution)/shard_map/all_to_all | solution.py:274
  68.1 1.4 copy-start.3
  69.5 2.1 copy-start.1
  71.4 2.8 %copy-start.4 = (bf16[32,16,896]{2,1,0:T(8,128)(2,1)}, bf16[32,16,896]{2,1,0:T(8,128)(2,1)S(1)}, u32[]{:S(2)}) copy-start(bf16[32,16,896]{2,1,0:T(8,128)(2,1)S(1)} %get-tuple-element.28) | copy-start | bytes 2752516
  71.6 2.6 copy-start.5
  71.6 2.6 copy-start.6
  184.7 4.0 %copy-start.2 = (bf16[3,640,1024]{2,1,0:T(8,128)(2,1)S(1)}, bf16[3,640,1024]{2,1,0:T(8,128)(2,1)}, u32[]{:S(2)}) copy-start(bf16[3,640,1024]{2,1,0:T(8,128)(2,1)} %line_activations.1.b_ref.a_ref) | copy-start | bytes 11796484
  198.7 58.5 %all-to-all-start.1 = ((bf16[32,40,896]{2,1,0:T(8,128)(2,1)}), bf16[32,40,896]{2,1,0:T(8,128)(2,1)}, u32[]{:S(2)}, u32[]{:S(2)}) async-start(bf16[32,40,896]{2,1,0:T(8,128)(2,1)} %pad_maximum_fusion.4), calls=%async_computation.1 | async-start | bytes 4587520 | tf_op jit(solution)/shard_map/all_to_all | solution.py:303
  205.4 11.4 %copy-start = (bf16[2,896,1024]{2,1,0:T(8,128)(2,1)S(1)}, bf16[2,896,1024]{2,1,0:T(8,128)(2,1)}, u32[]{:S(2)}) copy-start(bf16[2,896,1024]{2,1,0:T(8,128)(2,1)} %w_ref.1) | copy-start | bytes 11010052
  235.9 23.0 %copy-start.7 = (s32[128,1]{0,1:T(1,128)S(1)}, s32[128,1]{0,1:T(1,128)}, u32[]{:S(2)}) copy-start(s32[128,1]{0,1:T(1,128)} %param.12) | copy-start | bytes 1540
  260.0 1.8 copy-start.8

commit v5 on v4

--- a/solution.py
+++ b/solution.py
@@ -85,7 +85,7 @@
     )(a, b, w, m, v)
 
 
-SKEW = 2
+SKEW = 1
 
 
 def line_body(n, chunk, count, splits, ab_ref, g_ref, out_ref, sums, got, send, recv):

time: 265 us -> 309 us (1.17)
  Pallas kernels: 137 us -> 178 us
    pallas_call x1, Pallas kernels: 106 us -> 148 us  [line_activations(): pl.pallas_call(functools.partial(line_body, n, chunk, count, splits), out...]
  transfers between devices with their start and end apart: 2 -> 2, of which waited for: 2 -> 2; matrix products, arithmetic and copies ran while one was open for 2% -> 2% of each run, Pallas kernels for 12% -> 10%
where the time goes in v5:
time: 309 us; the launch traced here: 308 us
  Pallas kernels  178 us (58%)
  waiting for transfers between devices  70.1 us (23%)
  matrix products  18.5 us (6%)
  starting transfers between devices  15.5 us (5%)
  local copies, waits for them, and re-layouts  14.4 us (5%)
  other arithmetic  10.8 us (3%)
    pallas_call x1, Pallas kernels, line_activations(): pl.pallas_call(functools.partial(line_body, n, chunk, count, splits), out...  148 us
    all_to_all x1, waiting for transfers between devices, shards(): lax.all_to_all(packed.reshape(peers, span, block), BOTH, split_axis=0, co...  48.9 us
    pallas_call x2, Pallas kernels, grad_adam(): pl.pallas_call(functools.partial(adam_body, scale), grid=(parts, width //...  30.4 us
    all_to_all x1, waiting for transfers between devices, shards(): back = lax.all_to_all(parts, BOTH, split_axis=0, concat_axis=0, tiled=True)  21.2 us
    all_to_all x1, starting transfers between devices, shards(): back = lax.all_to_all(parts, BOTH, split_axis=0, concat_axis=0, tiled=True)  8.18 us
    all_to_all x1, starting transfers between devices, shards(): lax.all_to_all(packed.reshape(peers, span, block), BOTH, split_axis=0, co...  7.3 us
  transfers between devices with their start and end apart: 2, of which 2 were waited for; matrix products, arithmetic and copies ran while one was open for 2% of the time, Pallas kernels for 10%

profile of v5, /device:TPU:0, one launch (start us, length us, event | category | flops | bytes accessed | tf_op | source)
XLA Modules:
  0.0 308.0 jit_solution(15118729062346314596)
XLA Ops:
  1.5 1.4 multiply_convert_fusion
  3.8 2.0 convolution_convert_fusion
  6.0 1.7 pad_maximum_fusion.3
  7.7 7.3 %all-to-all-start = ((bf16[32,40,896]{2,1,0:T(8,128)(2,1)}), bf16[32,40,896]{2,1,0:T(8,128)(2,1)S(1)}, u32[]{:S(2)}, u32[]{:S(2)}) async-start(bf16[32,40,896]{2,1,0:T(8,128)(2,1)} %bitcast.51), calls=%async_computation | async-start | bytes 4587520 | tf_op jit(solution)/shard_map/all_to_all | solution.py:274
  15.0 4.3 %slice_bitcast_fusion.1 = (bf16[896,1024]{1,0:T(8,128)(2,1)}, bf16[896,1024]{1,0:T(8,128)(2,1)}) fusion(bf16[2,896,1024]{2,1,0:T(8,128)(2,1)} %w_ref.1), kind=kLoop, calls=%fused_computation.15 | loop fusion | bytes 7340032 | tf_op jit(solution)/shard_map/squeeze | solution.py:286
  19.2 48.9 %all-to-all-done = bf16[32,40,896]{2,1,0:T(8,128)(2,1)S(1)} async-done(((bf16[32,40,896]{2,1,0:T(8,128)(2,1)}), bf16[32,40,896]{2,1,0:T(8,128)(2,1)S(1)}, u32[]{:S(2)}, u32[]{:S(2)}) %all-to-all-start) | async-done | bytes 2293792 | tf_op jit(solution)/shard_map/all_to_all | solution.py:274
  68.3 1.2 copy-done.3
  69.6 1.7 fusion.38
  71.6 2.6 convolution_convert_fusion.2.g_ref
  74.2 4.3 %convolution_convert_fusion.1.ab_ref = bf16[640,2048]{1,0:T(8,128)(2,1)} fusion(bf16[896,1024]{1,0:T(8,128)(2,1)S(1)} %copy-done.6, bf16[896,1024]{1,0:T(8,128)(2,1)S(1)} %copy-done.5, bf16[128,896]{1,0:T(8,128)(2,1)S(1)} %reshape.83, bf16[512,896]{1,0:T(8,128)(2,1)S(1)} %bitcast.60), kind=kOutput, calls=%fused_computation.2 | convolution fusion | flops 2359754752 | bytes 7438336 | tf_op jit(solution)/shard_map/dot_general | solution.py:287
  78.5 147.6 %line_activations.1.b_ref.a_ref = bf16[3,640,1024]{2,1,0:T(8,128)(2,1)} custom-call(bf16[640,2048]{1,0:T(8,128)(2,1)} %convolution_convert_fusion.1.ab_ref, bf16[640,1024]{1,0:T(8,128)(2,1)} %convolution_convert_fusion.2.g_ref), custom_call_target="tpu_custom_call" | custom-call | flops 19660800 | bytes 7864320 | tf_op jit(solution)/shard_map/line_activations/pallas_call | solution.py:228
  226.1 3.0 convolution_convert_fusion.3
  229.1 1.0 slice.100
  230.3 2.9 fusion.8
  233.9 1.0 slice.101
  235.7 1.0 reshape.89
  236.7 3.4 %pad_maximum_fusion.4 = bf16[32,40,896]{2,1,0:T(8,128)(2,1)} fusion(bf16[32,4,896]{2,1,0:T(4,128)(2,1)S(1)} %reshape.89, bf16[32,4,896]{2,1,0:T(4,128)(2,1)} %reshape.88, bf16[32,16,896]{2,1,0:T(8,128)(2,1)} %bitcast.67, bf16[32,16,896]{2,1,0:T(8,128)(2,1)} %bitcast.66), kind=kLoop, calls=%fused_computation.8 | loop fusion | flops 9175040 | bytes 4587520 | tf_op jit(solution)/shard_map/concatenate | solution.py:298
  240.0 8.2 %all-to-all-start.1 = ((bf16[32,40,896]{2,1,0:T(8,128)(2,1)}), bf16[32,40,896]{2,1,0:T(8,128)(2,1)}, u32[]{:S(2)}, u32[]{:S(2)}) async-start(bf16[32,40,896]{2,1,0:T(8,128)(2,1)} %pad_maximum_fusion.4), calls=%async_computation.1 | async-start | bytes 4587520 | tf_op jit(solution)/shard_map/all_to_all | solution.py:303
  248.2 1.3 fusion.14.b_ref
  249.5 11.3 %grad_adam.3 = (bf16[1,1024,896]{2,1,0:T(8,128)(2,1)}, f32[1,1024,896]{2,1,0:T(8,128)}, f32[1,1024,896]{2,1,0:T(8,128)}) custom-call(bf16[3,640,1024]{2,1,0:T(8,128)(2,1)} %line_activations.1.b_ref.a_ref, bf16[1,640,896]{2,1,0:T(8,128)(2,1)S(1)} %fusion.14.b_ref, bf16[1,1024,896]{2,1,0:T(8,128)(2,1)S(1)} %bitcast.50, f32[1,1024,896]{2,1,0:T(8,128)} %bitcast.64, ...), custom_call_target="tpu_custom_call" | custom-call | flops 1174405120 | bytes 18350080 | tf_op jit(solution)/shard_map/grad_adam/pallas_call | solution.py:64
  261.0 19.0 %grad_adam.2 = (bf16[2,896,1024]{2,1,0:T(8,128)(2,1)}, f32[2,896,1024]{2,1,0:T(8,128)}, f32[2,896,1024]{2,1,0:T(8,128)}) custom-call(bf16[1,640,896]{2,1,0:T(8,128)(2,1)S(1)} %fusion.15.a_ref, bf16[3,640,1024]{2,1,0:T(8,128)(2,1)} %line_activations.1.b_ref.a_ref, bf16[2,896,1024]{2,1,0:T(8,128)(2,1)S(1)} %copy-done, f32[2,896,1024]{2,1,0:T(8,128)} %m_ref.1, ...), custom_call_target="tpu_custom_call" | custom-call | flops 2348810240 | bytes 36700160 | tf_op jit(solution)/shard_map/grad_adam/pallas_call | solution.py:64
  280.0 21.2 %all-to-all-done.1 = bf16[32,40,896]{2,1,0:T(8,128)(2,1)} async-done(((bf16[32,40,896]{2,1,0:T(8,128)(2,1)}), bf16[32,40,896]{2,1,0:T(8,128)(2,1)}, u32[]{:S(2)}, u32[]{:S(2)}) %all-to-all-start.1) | async-done | bytes 2293792 | tf_op jit(solution)/shard_map/all_to_all | solution.py:303
  301.2 1.8 fusion.37
  305.9 1.1 fusion.7
  (39 shorter events, 8.0 us)
Async XLA Ops:
  7.7 60.4 %all-to-all-start = ((bf16[32,40,896]{2,1,0:T(8,128)(2,1)}), bf16[32,40,896]{2,1,0:T(8,128)(2,1)S(1)}, u32[]{:S(2)}, u32[]{:S(2)}) async-start(bf16[32,40,896]{2,1,0:T(8,128)(2,1)} %bitcast.51), calls=%async_computation | async-start | bytes 4587520 | tf_op jit(solution)/shard_map/all_to_all | solution.py:274
  68.1 1.4 copy-start.3
  69.5 2.1 copy-start.1
  71.4 2.8 copy-start.4
  71.6 2.6 copy-start.5
  71.6 2.6 copy-start.6
  226.0 4.0 %copy-start.2 = (bf16[3,640,1024]{2,1,0:T(8,128)(2,1)S(1)}, bf16[3,640,1024]{2,1,0:T(8,128)(2,1)}, u32[]{:S(2)}) copy-start(bf16[3,640,1024]{2,1,0:T(8,128)(2,1)} %line_activations.1.b_ref.a_ref) | copy-start | bytes 11796484
  240.0 61.2 %all-to-all-start.1 = ((bf16[32,40,896]{2,1,0:T(8,128)(2,1)}), bf16[32,40,896]{2,1,0:T(8,128)(2,1)}, u32[]{:S(2)}, u32[]{:S(2)}) async-start(bf16[32,40,896]{2,1,0:T(8,128)(2,1)} %pad_maximum_fusion.4), calls=%async_computation.1 | async-start | bytes 4587520 | tf_op jit(solution)/shard_map/all_to_all | solution.py:303
  249.5 11.4 %copy-start = (bf16[2,896,1024]{2,1,0:T(8,128)(2,1)S(1)}, bf16[2,896,1024]{2,1,0:T(8,128)(2,1)}, u32[]{:S(2)}) copy-start(bf16[2,896,1024]{2,1,0:T(8,128)(2,1)} %w_ref.1) | copy-start | bytes 11010052
  280.0 23.0 %copy-start.7 = (s32[128,1]{0,1:T(1,128)S(1)}, s32[128,1]{0,1:T(1,128)}, u32[]{:S(2)}) copy-start(s32[128,1]{0,1:T(1,128)} %param.12) | copy-start | bytes 1540
  304.1 1.8 copy-start.8
